TPU v7x, 512 devices: a whole 4x4x16 slice. The times are simulated.
512 devices in a mesh: band: 8 (over x, core), sub: 64 (over z, y).
Axes of the slice: x: 4, y: 4, z: 16, core: 2. Of those that a mesh axis runs over, the one named last changes fastest.
Arguments:
- spectra: bfloat16 [64, 64, 128, 256], P('sub', None, 'band'), parts along dimension 2, may hold values from -500 to 500
- bin_freqs: float32 [128], P('band'), parts along dimension 0, may hold values from 0.5 to 5
- station_offsets: float32 [2, 128], replicated, may hold values from -1 to 1
- beam_grid: int32 [64], replicated, may hold values from 0 to 255, as said below
- owner_subarrays: int32 [64, 4], replicated, may hold values from 0 to 63, as said below
- pair_slots: int32 [64, 6, 2], P('sub'), may hold values from 0 to 3, as said below
- pair_count: int32 [64], P('sub'), may hold values from 1 to 6, as said below
Outputs:
- power: float32 [384, 512, 64], P('sub', 'band'), parts along dimension 1
There are 8 independent parts, one for each index of `band`. A program takes and returns all parts, laid end to end along the dimension named above; an argument that names none is the same for every part. Nothing has to cross between parts.
Inputs may be any that keep to these rules, and one draw needn't show every extreme that they name: `beam_grid`: within each part 64 distinct nodes; nodes 0 and 255 are always among them. `owner_subarrays`: each owner's row holds 4 distinct subarrays; every subarray is held by some owner. `pair_slots`: each owner's slots name distinct unordered pairs of two different positions, first below second. `pair_count`: one owner has all 6 slots live.
All inputs are finite; a program needn't handle non-finite values.
Results may differ from a plain program's by a relative error of at most 0.0026.
Values may be sent and summed in bfloat16 or wider, within the bound.
No kernel may reach another device: no remote copies, remote signals or barrier semaphores. Data moves between devices by JAX's collectives and lax.ppermute only.
A program may use at most 64 MiB of HBM per device.

v0:
```python
import math

import jax
import jax.numpy as jnp
from jax import lax
from jax.sharding import PartitionSpec as P

slow_step = 0.04
eps = 1e-06


def steering(bin_freqs, station_offsets, beam_grid):
    slow_x = ((beam_grid % 16).astype(jnp.float32) - 7.5) * slow_step
    slow_y = ((beam_grid // 16).astype(jnp.float32) - 7.5) * slow_step
    delay = (
        slow_x[:, None] * station_offsets[0][None, :]
        + slow_y[:, None] * station_offsets[1][None, :]
    )
    phase = 2.0 * math.pi * bin_freqs[:, None, None] * delay[None, :, :]
    factor = station_offsets.shape[1] ** (-0.5)
    cosine = jnp.swapaxes(jnp.cos(phase), 1, 2) * factor
    sine = jnp.swapaxes(jnp.sin(phase), 1, 2) * factor
    upper = jnp.concatenate([cosine, -sine], axis=2)
    lower = jnp.concatenate([sine, cosine], axis=2)
    return jnp.concatenate([upper, lower], axis=1).astype(jnp.bfloat16)


def pair_power(held, pair, divisor):
    first = lax.dynamic_index_in_dim(held, pair[0], 1, keepdims=False)
    second = lax.dynamic_index_in_dim(held, pair[1], 1, keepdims=False)
    product = jnp.einsum("rnb,rnc->nbc", first, second, preferred_element_type=jnp.float32)
    half = product.shape[-1] // 2
    real = product[:, :half, :half] + product[:, half:, half:]
    imag = product[:, half:, :half] - product[:, :half, half:]
    return jnp.sum(real * real + imag * imag, axis=0) / divisor


def shards(spectra, bin_freqs, station_offsets, beam_grid, owner_subarrays, pair_slots, pair_count):
    local_records = spectra.shape[0]
    records = lax.axis_size("sub") * local_records
    bins = spectra.shape[2]
    stations = spectra.shape[3] // 2
    owners = owner_subarrays.shape[0]
    held_count = owner_subarrays.shape[1]
    energy = jnp.sum(jnp.square(spectra.astype(jnp.float32)), axis=(0, 2))
    energy = energy[:, :stations] + energy[:, stations:]
    energy = lax.psum(energy, "sub")
    scale = lax.rsqrt(energy / (records * bins) + eps)
    scale = jnp.concatenate([scale, scale], axis=1)
    whitened = (spectra.astype(jnp.float32) * scale[None, :, None, :]).astype(jnp.bfloat16)
    matrix = steering(bin_freqs, station_offsets, beam_grid)
    flat_ids = owner_subarrays.reshape(-1)
    beams = jnp.einsum(
        "rqns,nsb->rqnb", whitened, matrix, preferred_element_type=jnp.float32
    ).astype(jnp.bfloat16)
    outgoing = jnp.take(beams, flat_ids, axis=1)
    outgoing = outgoing.reshape(local_records, owners, held_count, bins, beams.shape[-1])
    held = lax.all_to_all(outgoing, "sub", split_axis=1, concat_axis=0, tiled=True)
    held = held.reshape(records, held_count, bins, held.shape[-1])
    slots = pair_slots[0]
    count = pair_count[0]
    half = held.shape[-1] // 2
    divisor = bins * records
    empty = jnp.zeros((slots.shape[0], half, half), jnp.float32)

    def add_slot(index, total):
        return lax.dynamic_update_index_in_dim(
            total, pair_power(held, slots[index], divisor), index, 0
        )

    power = lax.fori_loop(0, count, add_slot, empty)
    return power


def solution(mesh):
    return jax.shard_map(
        shards,
        mesh=mesh,
        in_specs=(
            P("sub", None, "band", None),
            P("band"),
            P(),
            P(),
            P(),
            P("sub", None, None),
            P("sub"),
        ),
        out_specs=P("sub", "band", None),
        check_vma=False,
    )
```

profile of v0, /device:TPU:120, one launch (start us, length us, event | category | flops | bytes accessed | tf_op | source)
XLA Modules:
  0.0 378.0 jit_solution(7437360073528418310)
XLA Ops:
  0.0 0.8 copy.16
  0.8 0.7 compare_and_fusion
  1.5 0.8 slice_bitcast_fusion.1
  2.3 0.7 fusion.30
  2.9 0.7 broadcast_multiply_fusion
  3.6 1.3 fusion.11
  4.9 276.2 %psum.7 = f32[64,128]{1,0:T(8,128)S(1)} all-reduce(f32[64,128]{1,0:T(8,128)S(1)} %slice_add_fusion.1), channel_id=1, replica_groups=mesh['band'=8,'sub'=64] {'sub'}, use_global_device_ids=true, to_apply=%region_1.0 | all-reduce | flops 8192 | bytes 65536 | tf_op jit(solution)/shard_map/psum | solution.py:47
  281.1 0.0 copy-done
  281.1 0.1 fusion.26
  281.3 0.1 multiply_add_fusion
  281.4 4.2 %fusion.18 = (bf16[16,128,64]{2,1,0:T(8,128)(2,1)S(1)}, bf16[16,128,64]{2,1,0:T(8,128)(2,1)S(1)}, bf16[16,128,64]{2,1,0:T(8,128)(2,1)S(1)}) fusion(f32[128,64]{1,0:T(8,128)S(1)} %multiply_add_fusion, f32[16]{0:T(128)S(1)} %broadcast_multiply_fusion), kind=kLoop, calls=%fused_computation.28 | loop fusion | flops 917504 | bytes 819264 | tf_op jit(solution)/shard_map/convert.5
  285.6 0.8 fusion.10
  286.4 0.2 copy.17
  286.6 0.1 reshape.139
  286.7 0.1 copy.14
  286.8 0.8 gather_fusion
  287.7 1.2 broadcast_select_fusion
  288.9 20.4 %all-to-all-start = ((bf16[1,64,4,16,128]{4,3,2,0,1:T(8,128)(2,1)}), bf16[1,64,4,16,128]{4,3,2,0,1:T(8,128)(2,1)S(1)}, u32[]{:S(2)}, u32[]{:S(2)}) async-start(bf16[1,64,4,16,128]{4,3,2,0,1:T(8,128)(2,1)} %broadcast_select_fusion), calls=%async_computation | async-start | bytes 2097152 | tf_op jit(solution)/shard_map/all_to_all | solution.py:58
  309.3 31.5 %all-to-all-done = bf16[1,64,4,16,128]{4,3,2,0,1:T(8,128)(2,1)S(1)} async-done(((bf16[1,64,4,16,128]{4,3,2,0,1:T(8,128)(2,1)}), bf16[1,64,4,16,128]{4,3,2,0,1:T(8,128)(2,1)S(1)}, u32[]{:S(2)}, u32[]{:S(2)}) %all-to-all-start) | async-done | bytes 1048608 | tf_op jit(solution)/shard_map/all_to_all | solution.py:58
  340.8 0.7 copy.19
  341.5 0.0 copy-done.2
  341.5 35.8 %while.10 = (s32[]{:T(128)}, f32[6,64,64]{2,1,0:T(8,128)S(1)}, s32[]{:T(128)}, s32[6,2]{0,1:T(2,128)S(1)}, bf16[64,4,16,128]{3,0,2,1:T(8,128)(2,1)S(1)}, /*index=5*/s32[]{:T(128)}, s32[]{:T(128)}, s32[]{:T(128)}, s32[]{:T(128)}) while((s32[]{:T(128)}, f32[6,64,64]{2,1,0:T(8,128)S(1)}, s32[]{:T(128)}, s32[6,2]{0,1:T(2,128)S(1)}, ...), condition=%wide.region_4.5_spmd, body=%wide.region_2.4_spmd.sunk | while | flops 33947656 | bytes 2703603 | solution.py:71
  342.2 0.1 constant_dynamic-slice_fusion.2
  342.2 0.6 fusion.40
  346.6 0.4 fusion.41
  347.0 0.3 fusion.42
  348.0 0.1 constant_dynamic-slice_fusion.2
  348.1 0.6 fusion.40
  352.5 0.4 fusion.41
  352.9 0.3 fusion.42
  353.9 0.1 constant_dynamic-slice_fusion.2
  354.0 0.6 fusion.40
  358.3 0.4 fusion.41
  358.7 0.3 fusion.42
  359.7 0.1 constant_dynamic-slice_fusion.2
  359.8 0.6 fusion.40
  364.2 0.4 fusion.41
  364.6 0.3 fusion.42
  365.6 0.1 constant_dynamic-slice_fusion.2
  365.7 0.6 fusion.40
  370.1 0.4 fusion.41
  370.4 0.3 fusion.42
  371.4 0.1 constant_dynamic-slice_fusion.2
  371.5 0.6 fusion.40
  375.9 0.4 fusion.41
  376.3 0.3 fusion.42
  377.3 0.0 copy-start.1
  377.3 0.7 copy-done.1
  (14 shorter events, 0.1 us)
Async XLA Ops:
  0.0 281.1 %copy-start = (bf16[1,64,16,256]{3,2,1,0:T(8,128)(2,1)S(1)}, bf16[1,64,16,256]{3,2,1,0:T(8,128)(2,1)}, u32[]{:S(2)}) copy-start(bf16[1,64,16,256]{3,2,1,0:T(8,128)(2,1)} %param.9) | copy-start | bytes 1572868
  288.9 51.9 %all-to-all-start = ((bf16[1,64,4,16,128]{4,3,2,0,1:T(8,128)(2,1)}), bf16[1,64,4,16,128]{4,3,2,0,1:T(8,128)(2,1)S(1)}, u32[]{:S(2)}, u32[]{:S(2)}) async-start(bf16[1,64,4,16,128]{4,3,2,0,1:T(8,128)(2,1)} %broadcast_select_fusion), calls=%async_computation | async-start | bytes 2097152 | tf_op jit(solution)/shard_map/all_to_all | solution.py:58
  340.8 0.7 copy-start.2
  377.3 0.7 copy-start.1
where the time goes:
time: 376 us; the launch traced here: 378 us
  blocking collectives  276 us (73%)
  waiting for transfers between devices  31.5 us (8%)
  loops' own time  27.6 us (7%)
  starting transfers between devices  20.4 us (5%)
  other arithmetic  11.1 us (3%)
  local copies, waits for them, and re-layouts  8.15 us (2%)
    psum x1, blocking collectives, shards(): energy = lax.psum(energy, 'sub')  276 us
    all_to_all x1, waiting for transfers between devices, shards(): lax.all_to_all(outgoing, 'sub', split_axis=1, concat_axis=0, tiled=True)  31.5 us
    another operation x1, loops' own time, shards(): power = lax.fori_loop(0, count, add_slot, empty)  27.6 us
    all_to_all x1, starting transfers between devices, shards(): lax.all_to_all(outgoing, 'sub', split_axis=1, concat_axis=0, tiled=True)  20.4 us
  transfers between devices with their start and end apart: 1, of which 1 were waited for; matrix products, arithmetic and copies ran while one was open for 0% of the time, Pallas kernels for 0%

commit v1 on v0

--- a/solution.py
+++ b/solution.py
@@ -3,7 +3,11 @@
 import jax
 import jax.numpy as jnp
 from jax import lax
+from jax.sharding import Mesh
 from jax.sharding import PartitionSpec as P
+
+ROWS = 4
+SUB = ("z", "y")
 
 slow_step = 0.04
 eps = 1e-06
@@ -25,6 +29,19 @@
     return jnp.concatenate([upper, lower], axis=1).astype(jnp.bfloat16)
 
 
+def spread(block, size, axis):
+    copies = jnp.broadcast_to(block[None], (size, *block.shape))
+    return lax.all_to_all(copies, axis, 0, 0, tiled=True)
+
+
+def sum_over_sub(energy):
+    depth, rows = lax.axis_size("z"), lax.axis_size("y")
+    parts = energy.reshape(rows, -1, energy.shape[1])
+    group = jnp.sum(lax.all_to_all(parts, "y", 0, 0, tiled=True), axis=0)
+    group = jnp.sum(spread(group, depth, "z"), axis=0)
+    return spread(group, rows, "y").reshape(energy.shape)
+
+
 def pair_power(held, pair, divisor):
     first = lax.dynamic_index_in_dim(held, pair[0], 1, keepdims=False)
     second = lax.dynamic_index_in_dim(held, pair[1], 1, keepdims=False)
@@ -37,14 +54,14 @@
 
 def shards(spectra, bin_freqs, station_offsets, beam_grid, owner_subarrays, pair_slots, pair_count):
     local_records = spectra.shape[0]
-    records = lax.axis_size("sub") * local_records
+    records = (lax.axis_size("z") * lax.axis_size("y")) * local_records
     bins = spectra.shape[2]
     stations = spectra.shape[3] // 2
     owners = owner_subarrays.shape[0]
     held_count = owner_subarrays.shape[1]
     energy = jnp.sum(jnp.square(spectra.astype(jnp.float32)), axis=(0, 2))
     energy = energy[:, :stations] + energy[:, stations:]
-    energy = lax.psum(energy, "sub")
+    energy = sum_over_sub(energy)
     scale = lax.rsqrt(energy / (records * bins) + eps)
     scale = jnp.concatenate([scale, scale], axis=1)
     whitened = (spectra.astype(jnp.float32) * scale[None, :, None, :]).astype(jnp.bfloat16)
@@ -55,7 +72,7 @@
     ).astype(jnp.bfloat16)
     outgoing = jnp.take(beams, flat_ids, axis=1)
     outgoing = outgoing.reshape(local_records, owners, held_count, bins, beams.shape[-1])
-    held = lax.all_to_all(outgoing, "sub", split_axis=1, concat_axis=0, tiled=True)
+    held = lax.all_to_all(outgoing, SUB, split_axis=1, concat_axis=0, tiled=True)
     held = held.reshape(records, held_count, bins, held.shape[-1])
     slots = pair_slots[0]
     count = pair_count[0]
@@ -73,18 +90,20 @@
 
 
 def solution(mesh):
+    bands, subs = mesh.devices.shape
+    grid = Mesh(mesh.devices.reshape(bands, subs // ROWS, ROWS), ("band", "z", "y"))
     return jax.shard_map(
         shards,
-        mesh=mesh,
+        mesh=grid,
         in_specs=(
-            P("sub", None, "band", None),
+            P(SUB, None, "band", None),
             P("band"),
             P(),
             P(),
             P(),
-            P("sub", None, None),
-            P("sub"),
+            P(SUB, None, None),
+            P(SUB),
         ),
-        out_specs=P("sub", "band", None),
+        out_specs=P(SUB, "band", None),
         check_vma=False,
     )

time: 376 us -> 136 us (0.36)
  the two profiles are of different devices: /device:TPU:120 before, /device:TPU:338 now
where the time goes in v1:
time: 136 us; the launch traced here: 135 us
  waiting for transfers between devices  50.8 us (37%)
  starting transfers between devices  34.2 us (25%)
  loops' own time  26 us (19%)
  other arithmetic  11.7 us (9%)
  local copies, waits for them, and re-layouts  9.03 us (7%)
  matrix products  2.98 us (2%)
    all_to_all x1, waiting for transfers between devices, shards(): lax.all_to_all(outgoing, SUB, split_axis=1, concat_axis=0, tiled=True)  44.5 us
    another operation x1, loops' own time, shards(): power = lax.fori_loop(0, count, add_slot, empty)  26 us
    all_to_all x2, starting transfers between devices, spread(): return lax.all_to_all(copies, axis, 0, 0, tiled=True)  15.9 us
    all_to_all x1, starting transfers between devices, shards(): lax.all_to_all(outgoing, SUB, split_axis=1, concat_axis=0, tiled=True)  13.4 us
    all_to_all x2, waiting for transfers between devices, spread(): return lax.all_to_all(copies, axis, 0, 0, tiled=True)  6.29 us
    all_to_all x1, starting transfers between devices, sum_over_sub(): group = jnp.sum(lax.all_to_all(parts, 'y', 0, 0, tiled=True), axis=0)  4.8 us
    another operation x2, other arithmetic  4.33 us
    slice x6, local copies, waits for them, and re-layouts, pair_power(): first = lax.dynamic_index_in_dim(held, pair[0], 1, keepdims=False)  3.16 us
  transfers between devices with their start and end apart: 4, of which 3 were waited for; matrix products, arithmetic and copies ran while one was open for 6% of the time, Pallas kernels for 0%

profile of v1, /device:TPU:338, one launch (start us, length us, event | category | flops | bytes accessed | tf_op | source)
XLA Modules:
  0.0 134.8 jit_solution(14801727863192969395)
XLA Ops:
  0.0 1.3 fusion.11
  1.3 0.6 slice_add_fusion.1
  1.9 4.8 %all-to-all-start = ((f32[4,16,128]{2,1,0:T(8,128)}), f32[4,16,128]{2,1,0:T(8,128)S(1)}, u32[]{:S(2)}, u32[]{:S(2)}) async-start(f32[4,16,128]{2,1,0:T(8,128)} %bitcast.9), calls=%async_computation | async-start | bytes 65536 | tf_op jit(solution)/shard_map/all_to_all | solution.py:40
  6.7 0.8 copy.22
  7.5 0.7 compare_and_fusion
  8.1 0.8 slice_bitcast_fusion.1
  8.9 0.7 fusion.30
  9.6 0.1 reshape.151
  9.7 0.7 broadcast_multiply_fusion
  10.4 0.7 broadcast_in_dim.16
  11.0 11.1 %all-to-all-start.1 = ((f32[16,16,128]{2,1,0:T(8,128)}), f32[16,16,128]{2,1,0:T(8,128)S(1)}, u32[]{:S(2)}, u32[]{:S(2)}) async-start(f32[16,16,128]{2,1,0:T(8,128)} %broadcast_in_dim.16), calls=%async_computation.1 | async-start | bytes 262144 | tf_op jit(solution)/shard_map/all_to_all | solution.py:34
  22.1 0.1 multiply_add_fusion
  22.3 4.2 %fusion.18 = (bf16[16,128,64]{2,1,0:T(8,128)(2,1)S(1)}, bf16[16,128,64]{2,1,0:T(8,128)(2,1)S(1)}, bf16[16,128,64]{2,1,0:T(8,128)(2,1)S(1)}) fusion(f32[128,64]{1,0:T(8,128)S(1)} %multiply_add_fusion, f32[16]{0:T(128)S(1)} %broadcast_multiply_fusion), kind=kLoop, calls=%fused_computation.28 | loop fusion | flops 917504 | bytes 819264 | tf_op jit(solution)/shard_map/convert.5
  26.5 3.4 %all-to-all-done.1 = f32[16,16,128]{2,1,0:T(8,128)S(1)} async-done(((f32[16,16,128]{2,1,0:T(8,128)}), f32[16,16,128]{2,1,0:T(8,128)S(1)}, u32[]{:S(2)}, u32[]{:S(2)}) %all-to-all-start.1) | async-done | bytes 131104 | tf_op jit(solution)/shard_map/all_to_all | solution.py:34
  29.9 0.6 broadcast_in_dim.20
  30.5 4.8 %all-to-all-start.2 = ((f32[4,16,128]{2,1,0:T(8,128)}), f32[4,16,128]{2,1,0:T(8,128)S(1)}, u32[]{:S(2)}, u32[]{:S(2)}) async-start(f32[4,16,128]{2,1,0:T(8,128)} %broadcast_in_dim.20), calls=%async_computation.2 | async-start | bytes 65536 | tf_op jit(solution)/shard_map/all_to_all | solution.py:34
  35.3 0.1 copy.20
  35.4 2.9 %all-to-all-done.2 = f32[4,16,128]{2,1,0:T(8,128)S(1)} async-done(((f32[4,16,128]{2,1,0:T(8,128)}), f32[4,16,128]{2,1,0:T(8,128)S(1)}, u32[]{:S(2)}, u32[]{:S(2)}) %all-to-all-start.2) | async-done | bytes 32800 | tf_op jit(solution)/shard_map/all_to_all | solution.py:34
  38.4 0.1 fusion.26
  38.5 0.8 fusion.10
  39.3 0.2 copy.23
  39.5 0.8 gather_fusion
  40.4 1.2 broadcast_select_fusion
  41.6 13.4 %all-to-all-start.3 = ((bf16[1,64,4,16,128]{4,3,2,0,1:T(8,128)(2,1)}), bf16[1,64,4,16,128]{4,3,2,0,1:T(8,128)(2,1)S(1)}, u32[]{:S(2)}, u32[]{:S(2)}) async-start(bf16[1,64,4,16,128]{4,3,2,0,1:T(8,128)(2,1)} %broadcast_select_fusion), calls=%async_computation.3 | async-start | bytes 2097152 | tf_op jit(solution)/shard_map/all_to_all | solution.py:75
  55.0 44.5 %all-to-all-done.3 = bf16[1,64,4,16,128]{4,3,2,0,1:T(8,128)(2,1)S(1)} async-done(((bf16[1,64,4,16,128]{4,3,2,0,1:T(8,128)(2,1)}), bf16[1,64,4,16,128]{4,3,2,0,1:T(8,128)(2,1)S(1)}, u32[]{:S(2)}, u32[]{:S(2)}) %all-to-all-start.3) | async-done | bytes 1048608 | tf_op jit(solution)/shard_map/all_to_all | solution.py:75
  99.6 0.7 copy.25
  100.3 33.8 %while.10 = (s32[]{:T(128)}, f32[6,64,64]{2,1,0:T(8,128)S(1)}, s32[]{:T(128)}, s32[6,2]{0,1:T(2,128)S(1)}, bf16[64,4,16,128]{3,0,2,1:T(8,128)(2,1)S(1)}, /*index=5*/s32[]{:T(128)}, s32[]{:T(128)}, s32[]{:T(128)}, s32[]{:T(128)}) while((s32[]{:T(128)}, f32[6,64,64]{2,1,0:T(8,128)S(1)}, s32[]{:T(128)}, s32[6,2]{0,1:T(2,128)S(1)}, ...), condition=%wide.region_5.6_spmd, body=%wide.region_3.5_spmd.sunk | while | flops 33947656 | bytes 2703603 | solution.py:88
  100.9 0.1 constant_dynamic-slice_fusion.2
  101.0 0.5 fusion.40
  105.1 0.4 fusion.41
  105.4 0.3 fusion.42
  106.5 0.5 fusion.40
  110.6 0.4 fusion.41
  111.0 0.3 fusion.42
  112.0 0.1 constant_dynamic-slice_fusion.2
  112.1 0.5 fusion.40
  116.1 0.4 fusion.41
  116.5 0.3 fusion.42
  117.6 0.5 fusion.40
  121.7 0.4 fusion.41
  122.0 0.3 fusion.42
  123.1 0.5 fusion.40
  127.2 0.4 fusion.41
  127.6 0.3 fusion.42
  128.7 0.5 fusion.40
  132.7 0.4 fusion.41
  133.1 0.3 fusion.42
  134.1 0.7 copy-done.1
  (23 shorter events, 0.4 us)
Async XLA Ops:
  1.9 8.5 %all-to-all-start = ((f32[4,16,128]{2,1,0:T(8,128)}), f32[4,16,128]{2,1,0:T(8,128)S(1)}, u32[]{:S(2)}, u32[]{:S(2)}) async-start(f32[4,16,128]{2,1,0:T(8,128)} %bitcast.9), calls=%async_computation | async-start | bytes 65536 | tf_op jit(solution)/shard_map/all_to_all | solution.py:40
  11.0 18.9 %all-to-all-start.1 = ((f32[16,16,128]{2,1,0:T(8,128)}), f32[16,16,128]{2,1,0:T(8,128)S(1)}, u32[]{:S(2)}, u32[]{:S(2)}) async-start(f32[16,16,128]{2,1,0:T(8,128)} %broadcast_in_dim.16), calls=%async_computation.1 | async-start | bytes 262144 | tf_op jit(solution)/shard_map/all_to_all | solution.py:34
  22.2 16.1 %copy-start = (bf16[1,64,16,256]{3,2,1,0:T(8,128)(2,1)S(1)}, bf16[1,64,16,256]{3,2,1,0:T(8,128)(2,1)}, u32[]{:S(2)}) copy-start(bf16[1,64,16,256]{3,2,1,0:T(8,128)(2,1)} %param.9) | copy-start | bytes 1572868
  30.5 7.8 %all-to-all-start.2 = ((f32[4,16,128]{2,1,0:T(8,128)}), f32[4,16,128]{2,1,0:T(8,128)S(1)}, u32[]{:S(2)}, u32[]{:S(2)}) async-start(f32[4,16,128]{2,1,0:T(8,128)} %broadcast_in_dim.20), calls=%async_computation.2 | async-start | bytes 65536 | tf_op jit(solution)/shard_map/all_to_all | solution.py:34
  41.6 57.9 %all-to-all-start.3 = ((bf16[1,64,4,16,128]{4,3,2,0,1:T(8,128)(2,1)}), bf16[1,64,4,16,128]{4,3,2,0,1:T(8,128)(2,1)S(1)}, u32[]{:S(2)}, u32[]{:S(2)}) async-start(bf16[1,64,4,16,128]{4,3,2,0,1:T(8,128)(2,1)} %broadcast_select_fusion), calls=%async_computation.3 | async-start | bytes 2097152 | tf_op jit(solution)/shard_map/all_to_all | solution.py:75
  99.5 0.7 copy-start.2
  134.1 0.7 copy-start.1

commit v2 on v1

--- a/solution.py
+++ b/solution.py
@@ -1,8 +1,11 @@
+import functools
 import math
 
 import jax
 import jax.numpy as jnp
 from jax import lax
+from jax.experimental import pallas as pl
+from jax.experimental.pallas import tpu as pltpu
 from jax.sharding import Mesh
 from jax.sharding import PartitionSpec as P
 
@@ -42,14 +45,64 @@
     return spread(group, rows, "y").reshape(energy.shape)
 
 
-def pair_power(held, pair, divisor):
-    first = lax.dynamic_index_in_dim(held, pair[0], 1, keepdims=False)
-    second = lax.dynamic_index_in_dim(held, pair[1], 1, keepdims=False)
-    product = jnp.einsum("rnb,rnc->nbc", first, second, preferred_element_type=jnp.float32)
-    half = product.shape[-1] // 2
-    real = product[:, :half, :half] + product[:, half:, half:]
-    imag = product[:, half:, :half] - product[:, :half, half:]
-    return jnp.sum(real * real + imag * imag, axis=0) / divisor
+def pair_kernel(bins, slots_ref, count_ref, held_ref, power_ref, wide, most, rest, picked):
+    records, rows, width = held_ref.shape
+    half = width // 2
+    wide[...] = held_ref[...].astype(jnp.float32).reshape(wide.shape)
+    low = lax.broadcasted_iota(jnp.int32, (records, width), 1) < half
+    most[...] = jnp.zeros_like(most)
+    rest[...] = jnp.zeros_like(rest)
+    for n in range(bins):
+        held = [wide[pl.ds(h * bins + n, records, stride=rows), :] for h in range(4)]
+        turned = [pltpu.roll(x, half, 1) for x in held]
+        real = jnp.concatenate([jnp.where(low, held[0], turned[1]), held[2]], axis=1)
+        imag = jnp.concatenate([jnp.where(low, turned[0], held[1]), turned[2]], axis=1)
+        first = jnp.concatenate([real, imag], axis=0)[:, : 3 * half].astype(jnp.bfloat16)
+        second = [
+            jnp.concatenate([jnp.where(low, held[h], -held[h]), turned[h]], axis=0)
+            for h in range(1, 4)
+        ]
+        one = second[0].astype(jnp.bfloat16)
+        two = jnp.concatenate(second[1:], axis=1).astype(jnp.bfloat16)
+        dims = (((0,), (0,)), ((), ()))
+        cross = lax.dot_general(first, two, dims, preferred_element_type=jnp.float32)
+        most[...] += cross * cross
+        cross = lax.dot_general(first[:, :half], one, dims, preferred_element_type=jnp.float32)
+        rest[...] += cross * cross
+    picked[0, :half] = rest[:, :half] + rest[:, half:]
+    picked[1] = most[:, :half] + most[:, half:width]
+    picked[2] = most[:, width : width + half] + most[:, width + half :]
+    for p in range(power_ref.shape[0]):
+        row = pl.multiple_of(slots_ref[p, 0] * half, half)
+        power = picked[slots_ref[p, 1] - 1, pl.ds(row, half), :] / (bins * records)
+        power_ref[p] = jnp.where(p < count_ref[0], power, 0.0)
+
+
+def pair_powers(slots, count, held, bins):
+    records, rows, width = held.shape
+    half = width // 2
+    return pl.pallas_call(
+        functools.partial(pair_kernel, bins),
+        out_shape=jax.ShapeDtypeStruct((slots.shape[0], half, half), jnp.float32),
+        in_specs=[
+            pl.BlockSpec(memory_space=pltpu.SMEM),
+            pl.BlockSpec(memory_space=pltpu.SMEM),
+            pl.BlockSpec(memory_space=pltpu.VMEM),
+        ],
+        out_specs=pl.BlockSpec(memory_space=pltpu.VMEM),
+        scratch_shapes=[
+            pltpu.VMEM((records * rows, width), jnp.float32),
+            pltpu.VMEM((3 * half, 2 * width), jnp.float32),
+            pltpu.VMEM((half, width), jnp.float32),
+            pltpu.VMEM((3, 3 * half, half), jnp.float32),
+        ],
+        compiler_params=pltpu.CompilerParams(vmem_limit_bytes=32 * 1024 * 1024),
+        cost_estimate=pl.CostEstimate(
+            flops=2 * bins * 2 * records * 4 * half * 6 * half,
+            bytes_accessed=held.size * 2,
+            transcendentals=0,
+        ),
+    )(slots, count, held)
 
 
 def shards(spectra, bin_freqs, station_offsets, beam_grid, owner_subarrays, pair_slots, pair_count):
@@ -70,23 +123,11 @@
     beams = jnp.einsum(
         "rqns,nsb->rqnb", whitened, matrix, preferred_element_type=jnp.float32
     ).astype(jnp.bfloat16)
-    outgoing = jnp.take(beams, flat_ids, axis=1)
-    outgoing = outgoing.reshape(local_records, owners, held_count, bins, beams.shape[-1])
+    outgoing = beams.at[:, flat_ids].get(mode="promise_in_bounds")
+    outgoing = outgoing.reshape(local_records, owners, held_count * bins, beams.shape[-1])
     held = lax.all_to_all(outgoing, SUB, split_axis=1, concat_axis=0, tiled=True)
-    held = held.reshape(records, held_count, bins, held.shape[-1])
-    slots = pair_slots[0]
-    count = pair_count[0]
-    half = held.shape[-1] // 2
-    divisor = bins * records
-    empty = jnp.zeros((slots.shape[0], half, half), jnp.float32)
-
-    def add_slot(index, total):
-        return lax.dynamic_update_index_in_dim(
-            total, pair_power(held, slots[index], divisor), index, 0
-        )
-
-    power = lax.fori_loop(0, count, add_slot, empty)
-    return power
+    held = held.reshape(records, held_count * bins, held.shape[-1])
+    return pair_powers(pair_slots[0], pair_count, held, bins)
 
 
 def solution(mesh):

time: 136 us -> 116 us (0.85)
  the two profiles are of different devices: /device:TPU:338 before, /device:TPU:6 now
where the time goes in v2:
time: 116 us; the launch traced here: 115 us
  waiting for transfers between devices  68.9 us (59%)
  starting transfers between devices  28.3 us (24%)
  other arithmetic  7.69 us (7%)
  local copies, waits for them, and re-layouts  4.95 us (4%)
  Pallas kernels  3.78 us (3%)
    all_to_all x1, waiting for transfers between devices, shards(): lax.all_to_all(outgoing, SUB, split_axis=1, concat_axis=0, tiled=True)  52 us
    all_to_all x2, starting transfers between devices, spread(): return lax.all_to_all(copies, axis, 0, 0, tiled=True)  18.5 us
    all_to_all x2, waiting for transfers between devices, spread(): return lax.all_to_all(copies, axis, 0, 0, tiled=True)  14.5 us
    all_to_all x1, starting transfers between devices, shards(): lax.all_to_all(outgoing, SUB, split_axis=1, concat_axis=0, tiled=True)  5.33 us
    all_to_all x1, starting transfers between devices, sum_over_sub(): group = jnp.sum(lax.all_to_all(parts, 'y', 0, 0, tiled=True), axis=0)  4.46 us
    another operation x2, other arithmetic  4.33 us
    pallas_call x1, Pallas kernels, pair_powers(): pl.pallas_call(functools.partial(pair_kernel, bins), out_shape=jax.ShapeD...  3.78 us
    all_to_all x1, waiting for transfers between devices, sum_over_sub(): group = jnp.sum(lax.all_to_all(parts, 'y', 0, 0, tiled=True), axis=0)  2.47 us
  transfers between devices with their start and end apart: 4, of which 4 were waited for; matrix products, arithmetic and copies ran while one was open for 6% of the time, Pallas kernels for 0%

profile of v2, /device:TPU:6, one launch (start us, length us, event | category | flops | bytes accessed | tf_op | source)
XLA Modules:
  0.0 115.2 jit_solution(6517575249601653561)
XLA Ops:
  0.0 1.3 %fusion.1 = f32[64,256]{1,0:T(8,128)S(1)} fusion(bf16[1,64,16,256]{3,2,1,0:T(8,128)(2,1)} %param.7), kind=kLoop, calls=%fused_computation.7 | loop fusion | flops 770048 | bytes 589824 | tf_op jit(solution)/shard_map/reduce_sum | solution.py:115
  1.3 0.6 slice_add_fusion
  1.9 4.5 %all-to-all-start = ((f32[4,16,128]{2,1,0:T(8,128)}), f32[4,16,128]{2,1,0:T(8,128)S(1)}, u32[]{:S(2)}, u32[]{:S(2)}) async-start(f32[4,16,128]{2,1,0:T(8,128)} %bitcast.3), calls=%async_computation | async-start | bytes 65536 | tf_op jit(solution)/shard_map/all_to_all | solution.py:43
  6.3 0.7 fusion.20
  7.0 0.8 slice_bitcast_fusion.1
  7.8 0.8 copy.21
  8.5 0.1 reshape.121
  8.7 0.7 broadcast_multiply_fusion
  9.3 2.5 %all-to-all-done = f32[4,16,128]{2,1,0:T(8,128)S(1)} async-done(((f32[4,16,128]{2,1,0:T(8,128)}), f32[4,16,128]{2,1,0:T(8,128)S(1)}, u32[]{:S(2)}, u32[]{:S(2)}) %all-to-all-start) | async-done | bytes 32800 | tf_op jit(solution)/shard_map/all_to_all | solution.py:43
  11.8 0.7 broadcast_in_dim.4
  12.5 15.2 %all-to-all-start.1 = ((f32[16,16,128]{2,1,0:T(8,128)}), f32[16,16,128]{2,1,0:T(8,128)S(1)}, u32[]{:S(2)}, u32[]{:S(2)}) async-start(f32[16,16,128]{2,1,0:T(8,128)} %broadcast_in_dim.4), calls=%async_computation.1 | async-start | bytes 262144 | tf_op jit(solution)/shard_map/all_to_all | solution.py:37
  27.7 0.0 copy-start
  27.7 0.1 multiply_add_fusion
  27.8 4.2 %fusion.8 = (bf16[16,128,64]{2,1,0:T(8,128)(2,1)S(1)}, bf16[16,128,64]{2,1,0:T(8,128)(2,1)S(1)}, bf16[16,128,64]{2,1,0:T(8,128)(2,1)S(1)}) fusion(f32[128,64]{1,0:T(8,128)S(1)} %multiply_add_fusion, f32[16]{0:T(128)S(1)} %broadcast_multiply_fusion), kind=kLoop, calls=%fused_computation.14 | loop fusion | flops 917504 | bytes 819264 | tf_op jit(solution)/shard_map/convert.5
  32.0 9.1 %all-to-all-done.1 = f32[16,16,128]{2,1,0:T(8,128)S(1)} async-done(((f32[16,16,128]{2,1,0:T(8,128)}), f32[16,16,128]{2,1,0:T(8,128)S(1)}, u32[]{:S(2)}, u32[]{:S(2)}) %all-to-all-start.1) | async-done | bytes 131104 | tf_op jit(solution)/shard_map/all_to_all | solution.py:37
  41.1 0.6 broadcast_in_dim.5
  41.8 3.3 %all-to-all-start.2 = ((f32[4,16,128]{2,1,0:T(8,128)}), f32[4,16,128]{2,1,0:T(8,128)S(1)}, u32[]{:S(2)}, u32[]{:S(2)}) async-start(f32[4,16,128]{2,1,0:T(8,128)} %broadcast_in_dim.5), calls=%async_computation.2 | async-start | bytes 65536 | tf_op jit(solution)/shard_map/all_to_all | solution.py:37
  45.1 5.4 %all-to-all-done.2 = f32[4,16,128]{2,1,0:T(8,128)S(1)} async-done(((f32[4,16,128]{2,1,0:T(8,128)}), f32[4,16,128]{2,1,0:T(8,128)S(1)}, u32[]{:S(2)}, u32[]{:S(2)}) %all-to-all-start.2) | async-done | bytes 32800 | tf_op jit(solution)/shard_map/all_to_all | solution.py:37
  50.5 0.0 copy-done
  50.5 0.1 fusion.16
  50.6 0.8 fusion
  51.5 0.2 copy.22
  51.6 1.8 %gather_fusion = bf16[256,16,128]{2,1,0:T(8,128)(2,1)} fusion(bf16[64,16,128]{2,1,0:T(8,128)(2,1)S(1)} %copy.22, s32[1024]{0:T(1024)S(1)} %pad_clamp_fusion), kind=kCustom, calls=%fused_computation | custom fusion | bytes 2098176 | tf_op jit(solution)/shard_map/gather | solution.py:126
  53.4 0.0 copy-start.1
  53.4 5.3 %all-to-all-start.3 = ((bf16[1,64,64,128]{3,2,0,1:T(8,128)(2,1)}), bf16[1,64,64,128]{3,2,0,1:T(8,128)(2,1)S(1)}, u32[]{:S(2)}, u32[]{:S(2)}) async-start(bf16[1,64,64,128]{3,2,0,1:T(8,128)(2,1)} %bitcast.11), calls=%async_computation.3 | async-start | bytes 2097152 | tf_op jit(solution)/shard_map/all_to_all | solution.py:128
  58.7 0.0 copy-done.1
  58.7 0.1 copy.24.slots_ref
  59.5 52.0 %all-to-all-done.3 = bf16[1,64,64,128]{3,2,0,1:T(8,128)(2,1)S(1)} async-done(((bf16[1,64,64,128]{3,2,0,1:T(8,128)(2,1)}), bf16[1,64,64,128]{3,2,0,1:T(8,128)(2,1)S(1)}, u32[]{:S(2)}, u32[]{:S(2)}) %all-to-all-start.3) | async-done | bytes 1048608 | tf_op jit(solution)/shard_map/all_to_all | solution.py:128
  111.4 3.8 %shard_map.73 = f32[6,64,64]{2,1,0:T(8,128)} custom-call(s32[6,2]{1,0:T(8,128)S(1)} %copy.24.slots_ref, s32[1]{0:T(128)S(6)} %copy.27.count_ref, bf16[64,64,128]{2,1,0:T(8,128)(2,1)S(1)} %bitcast.20), custom_call_target="tpu_custom_call" | custom-call | flops 402653184 | bytes 1048576 | tf_op jit(solution)/shard_map/pallas_call | solution.py:84
  (6 shorter events, 0.1 us)
Async XLA Ops:
  1.9 9.9 %all-to-all-start = ((f32[4,16,128]{2,1,0:T(8,128)}), f32[4,16,128]{2,1,0:T(8,128)S(1)}, u32[]{:S(2)}, u32[]{:S(2)}) async-start(f32[4,16,128]{2,1,0:T(8,128)} %bitcast.3), calls=%async_computation | async-start | bytes 65536 | tf_op jit(solution)/shard_map/all_to_all | solution.py:43
  12.5 28.7 %all-to-all-start.1 = ((f32[16,16,128]{2,1,0:T(8,128)}), f32[16,16,128]{2,1,0:T(8,128)S(1)}, u32[]{:S(2)}, u32[]{:S(2)}) async-start(f32[16,16,128]{2,1,0:T(8,128)} %broadcast_in_dim.4), calls=%async_computation.1 | async-start | bytes 262144 | tf_op jit(solution)/shard_map/all_to_all | solution.py:37
  27.7 22.8 %copy-start = (bf16[1,64,16,256]{3,2,1,0:T(8,128)(2,1)S(1)}, bf16[1,64,16,256]{3,2,1,0:T(8,128)(2,1)}, u32[]{:S(2)}) copy-start(bf16[1,64,16,256]{3,2,1,0:T(8,128)(2,1)} %param.7) | copy-start | bytes 1572868
  41.8 8.7 %all-to-all-start.2 = ((f32[4,16,128]{2,1,0:T(8,128)}), f32[4,16,128]{2,1,0:T(8,128)S(1)}, u32[]{:S(2)}, u32[]{:S(2)}) async-start(f32[4,16,128]{2,1,0:T(8,128)} %broadcast_in_dim.5), calls=%async_computation.2 | async-start | bytes 65536 | tf_op jit(solution)/shard_map/all_to_all | solution.py:37
  53.4 5.3 %copy-start.1 = (s32[1,6,2]{1,2,0:T(2,128)S(1)}, s32[1,6,2]{1,2,0:T(2,128)}, u32[]{:S(2)}) copy-start(s32[1,6,2]{1,2,0:T(2,128)} %param.12) | copy-start | bytes 148
  53.4 58.1 %all-to-all-start.3 = ((bf16[1,64,64,128]{3,2,0,1:T(8,128)(2,1)}), bf16[1,64,64,128]{3,2,0,1:T(8,128)(2,1)S(1)}, u32[]{:S(2)}, u32[]{:S(2)}) async-start(bf16[1,64,64,128]{3,2,0,1:T(8,128)(2,1)} %bitcast.11), calls=%async_computation.3 | async-start | bytes 2097152 | tf_op jit(solution)/shard_map/all_to_all | solution.py:128

commit v3 on v2

--- a/solution.py
+++ b/solution.py
@@ -10,7 +10,8 @@
 from jax.sharding import PartitionSpec as P
 
 ROWS = 4
-SUB = ("z", "y")
+ZL = 2
+SUB = ("zh", "zl", "y")
 
 slow_step = 0.04
 eps = 1e-06
@@ -38,36 +39,39 @@
 
 
 def sum_over_sub(energy):
-    depth, rows = lax.axis_size("z"), lax.axis_size("y")
-    parts = energy.reshape(rows, -1, energy.shape[1])
-    group = jnp.sum(lax.all_to_all(parts, "y", 0, 0, tiled=True), axis=0)
-    group = jnp.sum(spread(group, depth, "z"), axis=0)
-    return spread(group, rows, "y").reshape(energy.shape)
+    near = ("zl", "y")
+    size = lax.axis_size(near)
+    parts = energy.reshape(size, -1, energy.shape[1])
+    group = jnp.sum(lax.all_to_all(parts, near, 0, 0, tiled=True), axis=0).astype(jnp.bfloat16)
+    all_groups = spread(group, lax.axis_size(SUB), SUB).astype(jnp.float32)
+    return jnp.sum(all_groups.reshape(-1, *energy.shape), axis=0)
 
 
-def pair_kernel(bins, slots_ref, count_ref, held_ref, power_ref, wide, most, rest, picked):
-    records, rows, width = held_ref.shape
+def pair_kernel(bins, slots_ref, count_ref, held_ref, power_ref, turned_ref, most, rest, picked):
+    records, _, width = held_ref.shape
     half = width // 2
-    wide[...] = held_ref[...].astype(jnp.float32).reshape(wide.shape)
+    for h in range(4):
+        turned_ref[h] = jnp.swapaxes(held_ref[:, h * bins : (h + 1) * bins, :], 0, 1)
     low = lax.broadcasted_iota(jnp.int32, (records, width), 1) < half
     most[...] = jnp.zeros_like(most)
     rest[...] = jnp.zeros_like(rest)
     for n in range(bins):
-        held = [wide[pl.ds(h * bins + n, records, stride=rows), :] for h in range(4)]
-        turned = [pltpu.roll(x, half, 1) for x in held]
-        real = jnp.concatenate([jnp.where(low, held[0], turned[1]), held[2]], axis=1)
-        imag = jnp.concatenate([jnp.where(low, turned[0], held[1]), turned[2]], axis=1)
-        first = jnp.concatenate([real, imag], axis=0)[:, : 3 * half].astype(jnp.bfloat16)
+        held = [turned_ref[h, n] for h in range(4)]
+        rolled = [pltpu.roll(x, half, 1) for x in held]
+        real = jnp.concatenate([jnp.where(low, held[0], rolled[1]), held[2]], axis=1)
+        imag = jnp.concatenate([jnp.where(low, rolled[0], held[1]), rolled[2]], axis=1)
+        first = jnp.concatenate([real, imag], axis=0)[:, : 3 * half]
         second = [
-            jnp.concatenate([jnp.where(low, held[h], -held[h]), turned[h]], axis=0)
+            jnp.concatenate([jnp.where(low, held[h], -held[h]), rolled[h]], axis=0)
             for h in range(1, 4)
         ]
-        one = second[0].astype(jnp.bfloat16)
-        two = jnp.concatenate(second[1:], axis=1).astype(jnp.bfloat16)
+        two = jnp.concatenate(second[1:], axis=1)
         dims = (((0,), (0,)), ((), ()))
         cross = lax.dot_general(first, two, dims, preferred_element_type=jnp.float32)
         most[...] += cross * cross
-        cross = lax.dot_general(first[:, :half], one, dims, preferred_element_type=jnp.float32)
+        cross = lax.dot_general(
+            first[:, :half], second[0], dims, preferred_element_type=jnp.float32
+        )
         rest[...] += cross * cross
     picked[0, :half] = rest[:, :half] + rest[:, half:]
     picked[1] = most[:, :half] + most[:, half:width]
@@ -91,7 +95,7 @@
         ],
         out_specs=pl.BlockSpec(memory_space=pltpu.VMEM),
         scratch_shapes=[
-            pltpu.VMEM((records * rows, width), jnp.float32),
+            pltpu.VMEM((4, bins, records, width), jnp.bfloat16),
             pltpu.VMEM((3 * half, 2 * width), jnp.float32),
             pltpu.VMEM((half, width), jnp.float32),
             pltpu.VMEM((3, 3 * half, half), jnp.float32),
@@ -107,7 +111,7 @@
 
 def shards(spectra, bin_freqs, station_offsets, beam_grid, owner_subarrays, pair_slots, pair_count):
     local_records = spectra.shape[0]
-    records = (lax.axis_size("z") * lax.axis_size("y")) * local_records
+    records = lax.axis_size(SUB) * local_records
     bins = spectra.shape[2]
     stations = spectra.shape[3] // 2
     owners = owner_subarrays.shape[0]
@@ -132,7 +136,7 @@
 
 def solution(mesh):
     bands, subs = mesh.devices.shape
-    grid = Mesh(mesh.devices.reshape(bands, subs // ROWS, ROWS), ("band", "z", "y"))
+    grid = Mesh(mesh.devices.reshape(bands, subs // ROWS // ZL, ZL, ROWS), ("band", "zh", "zl", "y"))
     return jax.shard_map(
         shards,
         mesh=grid,

time: 116 us -> 111 us (0.957)
  waiting for transfers between devices: 68.9 us -> 67 us
  starting transfers between devices: 28.3 us -> 26.4 us
    all_to_all x2 -> x1, waiting for transfers between devices: 14.5 us -> 11.7 us  [spread(): return lax.all_to_all(copies, axis, 0, 0, tiled=True)]
    all_to_all x2 -> x1, starting transfers between devices: 18.5 us -> 15.8 us  [spread(): return lax.all_to_all(copies, axis, 0, 0, tiled=True)]
    all_to_all x1, starting transfers between devices: 4.46 us -> 5.82 us  [sum_over_sub(): lax.all_to_all(parts, near, 0, 0, tiled=True)]
  transfers between devices with their start and end apart: 4 -> 3, of which waited for: 4 -> 3; matrix products, arithmetic and copies ran while one was open for 6% -> 7% of each run, Pallas kernels for 0% -> 0%
where the time goes in v3:
time: 111 us; the launch traced here: 110 us
  waiting for transfers between devices  67 us (60%)
  starting transfers between devices  26.4 us (24%)
  other arithmetic  7.7 us (7%)
  local copies, waits for them, and re-layouts  4.34 us (4%)
  Pallas kernels  3.08 us (3%)
    all_to_all x1, waiting for transfers between devices, shards(): lax.all_to_all(outgoing, SUB, split_axis=1, concat_axis=0, tiled=True)  52 us
    all_to_all x1, starting transfers between devices, spread(): return lax.all_to_all(copies, axis, 0, 0, tiled=True)  15.8 us
    all_to_all x1, waiting for transfers between devices, spread(): return lax.all_to_all(copies, axis, 0, 0, tiled=True)  11.7 us
    all_to_all x1, starting transfers between devices, sum_over_sub(): lax.all_to_all(parts, near, 0, 0, tiled=True)  5.82 us
    all_to_all x1, starting transfers between devices, shards(): lax.all_to_all(outgoing, SUB, split_axis=1, concat_axis=0, tiled=True)  4.78 us
    another operation x2, other arithmetic  4.33 us
    all_to_all x1, waiting for transfers between devices, sum_over_sub(): lax.all_to_all(parts, near, 0, 0, tiled=True)  3.28 us
    pallas_call x1, Pallas kernels, pair_powers(): pl.pallas_call(functools.partial(pair_kernel, bins), out_shape=jax.ShapeD...  3.08 us
  transfers between devices with their start and end apart: 3, of which 3 were waited for; matrix products, arithmetic and copies ran while one was open for 7% of the time, Pallas kernels for 0%

profile of v3, /device:TPU:6, one launch (start us, length us, event | category | flops | bytes accessed | tf_op | source)
XLA Modules:
  0.0 110.2 jit_solution(4690273845900861187)
XLA Ops:
  0.0 1.3 %fusion.1 = f32[64,256]{1,0:T(8,128)S(1)} fusion(bf16[1,64,16,256]{3,2,1,0:T(8,128)(2,1)} %param.7), kind=kLoop, calls=%fused_computation.7 | loop fusion | flops 770048 | bytes 589824 | tf_op jit(solution)/shard_map/reduce_sum | solution.py:119
  1.3 0.6 fusion.18
  1.9 5.8 %all-to-all-start = ((f32[8,8,128]{2,1,0:T(8,128)}), f32[8,8,128]{2,1,0:T(8,128)S(1)}, u32[]{:S(2)}, u32[]{:S(2)}) async-start(f32[8,8,128]{2,1,0:T(8,128)} %fusion.18), calls=%async_computation | async-start | bytes 65536 | tf_op jit(solution)/shard_map/all_to_all | solution.py:45
  7.7 0.7 fusion.21
  8.4 0.8 slice_bitcast_fusion.1
  9.1 0.8 copy.21
  9.9 0.1 reshape.124
  10.0 0.7 broadcast_multiply_fusion
  10.7 3.3 %all-to-all-done = f32[8,8,128]{2,1,0:T(8,128)S(1)} async-done(((f32[8,8,128]{2,1,0:T(8,128)}), f32[8,8,128]{2,1,0:T(8,128)S(1)}, u32[]{:S(2)}, u32[]{:S(2)}) %all-to-all-start) | async-done | bytes 32800 | tf_op jit(solution)/shard_map/all_to_all | solution.py:45
  14.0 0.7 broadcast_in_dim.2
  14.7 15.8 %all-to-all-start.1 = ((bf16[64,8,128]{2,1,0:T(8,128)(2,1)}), bf16[64,8,128]{2,1,0:T(8,128)(2,1)S(1)}, u32[]{:S(2)}, u32[]{:S(2)}) async-start(bf16[64,8,128]{2,1,0:T(8,128)(2,1)} %broadcast_in_dim.2), calls=%async_computation.1 | async-start | bytes 262144 | tf_op jit(solution)/shard_map/all_to_all | solution.py:38
  30.5 0.0 copy-start
  30.5 0.1 multiply_add_fusion
  30.6 4.2 %fusion.8 = (bf16[16,128,64]{2,1,0:T(8,128)(2,1)S(1)}, bf16[16,128,64]{2,1,0:T(8,128)(2,1)S(1)}, bf16[16,128,64]{2,1,0:T(8,128)(2,1)S(1)}) fusion(f32[128,64]{1,0:T(8,128)S(1)} %multiply_add_fusion, f32[16]{0:T(128)S(1)} %broadcast_multiply_fusion), kind=kLoop, calls=%fused_computation.14 | loop fusion | flops 917504 | bytes 819264 | tf_op jit(solution)/shard_map/convert.6
  34.8 11.7 %all-to-all-done.1 = bf16[64,8,128]{2,1,0:T(8,128)(2,1)S(1)} async-done(((bf16[64,8,128]{2,1,0:T(8,128)(2,1)}), bf16[64,8,128]{2,1,0:T(8,128)(2,1)S(1)}, u32[]{:S(2)}, u32[]{:S(2)}) %all-to-all-start.1) | async-done | bytes 131104 | tf_op jit(solution)/shard_map/all_to_all | solution.py:38
  46.6 0.0 copy-done
  46.6 0.1 fusion.16
  46.8 0.8 fusion
  47.6 0.2 copy.22
  47.8 1.8 %gather_fusion = bf16[256,16,128]{2,1,0:T(8,128)(2,1)} fusion(bf16[64,16,128]{2,1,0:T(8,128)(2,1)S(1)} %copy.22, s32[1024]{0:T(1024)S(1)} %pad_clamp_fusion), kind=kCustom, calls=%fused_computation | custom fusion | bytes 2098176 | tf_op jit(solution)/shard_map/gather | solution.py:130
  49.5 0.0 copy-start.1
  49.5 4.8 %all-to-all-start.2 = ((bf16[1,64,64,128]{3,2,0,1:T(8,128)(2,1)}), bf16[1,64,64,128]{3,2,0,1:T(8,128)(2,1)S(1)}, u32[]{:S(2)}, u32[]{:S(2)}) async-start(bf16[1,64,64,128]{3,2,0,1:T(8,128)(2,1)} %bitcast.11), calls=%async_computation.2 | async-start | bytes 2097152 | tf_op jit(solution)/shard_map/all_to_all | solution.py:132
  54.3 0.0 copy-done.1
  54.3 0.1 copy.24.slots_ref
  55.1 52.0 %all-to-all-done.2 = bf16[1,64,64,128]{3,2,0,1:T(8,128)(2,1)S(1)} async-done(((bf16[1,64,64,128]{3,2,0,1:T(8,128)(2,1)}), bf16[1,64,64,128]{3,2,0,1:T(8,128)(2,1)S(1)}, u32[]{:S(2)}, u32[]{:S(2)}) %all-to-all-start.2) | async-done | bytes 1048608 | tf_op jit(solution)/shard_map/all_to_all | solution.py:132
  107.1 3.1 %shard_map.73 = f32[6,64,64]{2,1,0:T(8,128)} custom-call(s32[6,2]{1,0:T(8,128)S(1)} %copy.24.slots_ref, s32[1]{0:T(128)S(6)} %copy.27.count_ref, bf16[64,64,128]{2,1,0:T(8,128)(2,1)S(1)} %bitcast.24), custom_call_target="tpu_custom_call" | custom-call | flops 402653184 | bytes 1048576 | tf_op jit(solution)/shard_map/pallas_call | solution.py:88
  (6 shorter events, 0.1 us)
Async XLA Ops:
  1.9 12.1 %all-to-all-start = ((f32[8,8,128]{2,1,0:T(8,128)}), f32[8,8,128]{2,1,0:T(8,128)S(1)}, u32[]{:S(2)}, u32[]{:S(2)}) async-start(f32[8,8,128]{2,1,0:T(8,128)} %fusion.18), calls=%async_computation | async-start | bytes 65536 | tf_op jit(solution)/shard_map/all_to_all | solution.py:45
  14.7 31.9 %all-to-all-start.1 = ((bf16[64,8,128]{2,1,0:T(8,128)(2,1)}), bf16[64,8,128]{2,1,0:T(8,128)(2,1)S(1)}, u32[]{:S(2)}, u32[]{:S(2)}) async-start(bf16[64,8,128]{2,1,0:T(8,128)(2,1)} %broadcast_in_dim.2), calls=%async_computation.1 | async-start | bytes 262144 | tf_op jit(solution)/shard_map/all_to_all | solution.py:38
  30.5 16.2 %copy-start = (bf16[1,64,16,256]{3,2,1,0:T(8,128)(2,1)S(1)}, bf16[1,64,16,256]{3,2,1,0:T(8,128)(2,1)}, u32[]{:S(2)}) copy-start(bf16[1,64,16,256]{3,2,1,0:T(8,128)(2,1)} %param.7) | copy-start | bytes 1572868
  49.5 4.8 %copy-start.1 = (s32[1,6,2]{1,2,0:T(2,128)S(1)}, s32[1,6,2]{1,2,0:T(2,128)}, u32[]{:S(2)}) copy-start(s32[1,6,2]{1,2,0:T(2,128)} %param.12) | copy-start | bytes 148
  49.5 57.6 %all-to-all-start.2 = ((bf16[1,64,64,128]{3,2,0,1:T(8,128)(2,1)}), bf16[1,64,64,128]{3,2,0,1:T(8,128)(2,1)S(1)}, u32[]{:S(2)}, u32[]{:S(2)}) async-start(bf16[1,64,64,128]{3,2,0,1:T(8,128)(2,1)} %bitcast.11), calls=%async_computation.2 | async-start | bytes 2097152 | tf_op jit(solution)/shard_map/all_to_all | solution.py:132

commit v4 on v3

v4 whole, which is shorter than its diff:
```python
import functools
import math

import jax
import jax.numpy as jnp
import numpy as np
from jax import lax
from jax.experimental import pallas as pl
from jax.experimental.pallas import tpu as pltpu
from jax.sharding import PartitionSpec as P

COLUMNS = 4
NEAR = 8
FIRST = (8, 2)

slow_step = 0.04
eps = 1e-06


def steering(bin_freqs, station_offsets, beam_grid):
    slow_x = ((beam_grid % 16).astype(jnp.float32) - 7.5) * slow_step
    slow_y = ((beam_grid // 16).astype(jnp.float32) - 7.5) * slow_step
    delay = (
        slow_x[:, None] * station_offsets[0][None, :]
        + slow_y[:, None] * station_offsets[1][None, :]
    )
    phase = 2.0 * math.pi * bin_freqs[:, None, None] * delay[None, :, :]
    factor = station_offsets.shape[1] ** (-0.5)
    cosine = jnp.swapaxes(jnp.cos(phase), 1, 2) * factor
    sine = jnp.swapaxes(jnp.sin(phase), 1, 2) * factor
    upper = jnp.concatenate([cosine, -sine], axis=2)
    lower = jnp.concatenate([sine, cosine], axis=2)
    return jnp.concatenate([upper, lower], axis=1).astype(jnp.bfloat16)


def energy_parts(spectra, near):
    subarrays, _, width = spectra.shape
    values = spectra.astype(jnp.float32)
    real, imag = values[:, :, : width // 2], values[:, :, width // 2 :]
    energy = jnp.sum(real * real + imag * imag, axis=1)
    return energy.reshape(near, subarrays // near, width // 2)


def encode(energy):
    scaled = jnp.square(energy * (1.0 / 256.0))
    return jnp.square(scaled).astype(jnp.bfloat16)


def decode(code):
    return jnp.sqrt(jnp.sqrt(code.astype(jnp.float32))) * 256.0


def beam_kernel(count, ids_ref, code_ref, spectra_ref, matrix_ref, out_ref, made, turned, chunk, sems):
    bins, subarrays, width = spectra_ref.shape
    held = ids_ref.shape[1]
    steps, per_step = chunk.shape[0], chunk.shape[1]
    groups = decode(code_ref[...]).reshape(-1, subarrays, width // 2)
    scale = lax.rsqrt(jnp.sum(groups, axis=0) / count + eps)
    scale = jnp.concatenate([scale, scale], axis=1)
    for n in range(bins):
        white = (spectra_ref[n].astype(jnp.float32) * scale).astype(jnp.bfloat16)
        made[n] = jnp.dot(
            white, matrix_ref[n], preferred_element_type=jnp.float32
        ).astype(jnp.bfloat16)
    turned[...] = jnp.swapaxes(made[...], 0, 1)
    copies = []
    for step in range(steps):
        for own in range(per_step):
            for h in range(held):
                chunk[step, own, h * bins : (h + 1) * bins] = turned[
                    ids_ref[step * per_step + own, h]
                ]
        copies.append(
            pltpu.make_async_copy(
                chunk.at[step], out_ref.at[pl.ds(step * per_step, per_step)], sems.at[step]
            )
        )
        copies[-1].start()
    for copy in copies:
        copy.wait()


def outgoing_beams(ids, code, spectra, matrix, count):
    bins, subarrays, width = spectra.shape
    owners, held = ids.shape
    beams = matrix.shape[2]
    steps = 8
    smem = pl.BlockSpec(memory_space=pltpu.SMEM)
    vmem = pl.BlockSpec(memory_space=pltpu.VMEM)
    return pl.pallas_call(
        functools.partial(beam_kernel, count),
        out_shape=jax.ShapeDtypeStruct((owners, held * bins, beams), jnp.bfloat16),
        in_specs=[smem, vmem, vmem, vmem],
        out_specs=pl.BlockSpec(memory_space=pl.ANY),
        scratch_shapes=[
            pltpu.VMEM((bins, subarrays, beams), jnp.bfloat16),
            pltpu.VMEM((subarrays, bins, beams), jnp.bfloat16),
            pltpu.VMEM((steps, owners // steps, held * bins, beams), jnp.bfloat16),
            pltpu.SemaphoreType.DMA((steps,)),
        ],
        compiler_params=pltpu.CompilerParams(vmem_limit_bytes=32 * 1024 * 1024),
        cost_estimate=pl.CostEstimate(
            flops=2 * bins * subarrays * width * beams,
            bytes_accessed=2 * (spectra.size + owners * held * bins * beams),
            transcendentals=0,
        ),
    )(ids, code, spectra, matrix)


def pair_kernel(bins, slots_ref, count_ref, held_ref, power_ref, turned_ref, most, rest, picked, made, sems):
    records, _, width = held_ref.shape
    half = width // 2
    for h in range(4):
        turned_ref[h] = jnp.swapaxes(held_ref[:, h * bins : (h + 1) * bins, :], 0, 1)
    low = lax.broadcasted_iota(jnp.int32, (records, width), 1) < half
    most[...] = jnp.zeros_like(most)
    rest[...] = jnp.zeros_like(rest)
    for n in range(bins):
        held = [turned_ref[h, n] for h in range(4)]
        rolled = [pltpu.roll(x, half, 1) for x in held]
        real = jnp.concatenate([jnp.where(low, held[0], rolled[1]), held[2]], axis=1)
        imag = jnp.concatenate([jnp.where(low, rolled[0], held[1]), rolled[2]], axis=1)
        first = jnp.concatenate([real, imag], axis=0)[:, : 3 * half]
        second = [
            jnp.concatenate([jnp.where(low, held[h], -held[h]), rolled[h]], axis=0)
            for h in range(1, 4)
        ]
        two = jnp.concatenate(second[1:], axis=1)
        dims = (((0,), (0,)), ((), ()))
        cross = lax.dot_general(first, two, dims, preferred_element_type=jnp.float32)
        most[...] += cross * cross
        cross = lax.dot_general(
            first[:, :half], second[0], dims, preferred_element_type=jnp.float32
        )
        rest[...] += cross * cross
    picked[0, :half] = rest[:, :half] + rest[:, half:]
    picked[1] = most[:, :half] + most[:, half:width]
    picked[2] = most[:, width : width + half] + most[:, width + half :]
    copies = []
    for p in range(power_ref.shape[0]):
        row = pl.multiple_of(slots_ref[p, 0] * half, half)
        power = picked[slots_ref[p, 1] - 1, pl.ds(row, half), :] / (bins * records)
        made[p] = jnp.where(p < count_ref[0], power, 0.0)
        copies.append(pltpu.make_async_copy(made.at[p], power_ref.at[p], sems.at[p]))
        copies[-1].start()
    for copy in copies:
        copy.wait()


def pair_powers(slots, count, held, bins):
    records, rows, width = held.shape
    half = width // 2
    return pl.pallas_call(
        functools.partial(pair_kernel, bins),
        out_shape=jax.ShapeDtypeStruct((slots.shape[0], half, half), jnp.float32),
        in_specs=[
            pl.BlockSpec(memory_space=pltpu.SMEM),
            pl.BlockSpec(memory_space=pltpu.SMEM),
            pl.BlockSpec(memory_space=pltpu.VMEM),
        ],
        out_specs=pl.BlockSpec(memory_space=pl.ANY),
        scratch_shapes=[
            pltpu.VMEM((4, bins, records, width), jnp.bfloat16),
            pltpu.VMEM((3 * half, 2 * width), jnp.float32),
            pltpu.VMEM((half, width), jnp.float32),
            pltpu.VMEM((3, 3 * half, half), jnp.float32),
            pltpu.VMEM((slots.shape[0], half, half), jnp.float32),
            pltpu.SemaphoreType.DMA((slots.shape[0],)),
        ],
        compiler_params=pltpu.CompilerParams(vmem_limit_bytes=32 * 1024 * 1024),
        cost_estimate=pl.CostEstimate(
            flops=2 * bins * 2 * records * 4 * half * 6 * half,
            bytes_accessed=held.size * 2,
            transcendentals=0,
        ),
    )(slots, count, held)


def exchange(blocks, groups):
    return lax.all_to_all(
        blocks, "sub", split_axis=0, concat_axis=0, tiled=True, axis_index_groups=groups
    )


def shards(spectra, bin_freqs, station_offsets, beam_grid, owner_subarrays, pair_slots, pair_count):
    spectra = spectra[0]
    bins = spectra.shape[1]
    records = lax.axis_size("sub")
    grid = np.arange(records).reshape(-1, COLUMNS)
    order = np.roll(grid, (-FIRST[0], -FIRST[1]), (0, 1)).reshape(-1)
    wide = [order.tolist()]
    near = order.reshape(-1, NEAR).tolist()
    parts = exchange(energy_parts(spectra, NEAR), near)
    group = jnp.sum(parts, axis=0)
    group, spectra, bin_freqs, station_offsets, beam_grid, owner_subarrays = lax.optimization_barrier(
        (group, spectra, bin_freqs, station_offsets, beam_grid, owner_subarrays)
    )
    code = encode(group)
    code = exchange(jnp.broadcast_to(code[None], (records, *code.shape)), wide)
    matrix = steering(bin_freqs, station_offsets, beam_grid)
    owners = owner_subarrays.reshape(-1, COLUMNS, owner_subarrays.shape[1])
    owners = jnp.roll(owners, (-FIRST[0], -FIRST[1]), (0, 1)).reshape(owner_subarrays.shape)
    outgoing = outgoing_beams(owners, code, jnp.swapaxes(spectra, 0, 1), matrix, records * bins)
    held = exchange(outgoing, wide)
    return pair_powers(pair_slots[0], pair_count, held, bins)


def solution(mesh):
    return jax.shard_map(
        shards,
        mesh=mesh,
        in_specs=(
            P("sub", None, "band", None),
            P("band"),
            P(),
            P(),
            P(),
            P("sub", None, None),
            P("sub"),
        ),
        out_specs=P("sub", "band", None),
        check_vma=False,
    )
```

time: 111 us -> 104 us (0.937)
  waiting for transfers between devices: 67 us -> 41.8 us
  starting transfers between devices: 26.4 us -> 37 us
  blocking collectives: 0 us -> 10.3 us
  local copies, waits for them, and re-layouts: 4.34 us -> 1.35 us
  Pallas kernels: 3.08 us -> 5.68 us
  other arithmetic: 7.7 us -> 6.31 us
    all_to_all x3 -> x2, waiting for transfers between devices: 67 us -> 41.8 us  [exchange(): lax.all_to_all(blocks, 'sub', split_axis=0, concat_axis=0, tiled=True, ax...]
    all_to_all x3 -> x2, starting transfers between devices: 26.4 us -> 37 us  [exchange(): lax.all_to_all(blocks, 'sub', split_axis=0, concat_axis=0, tiled=True, ax...]
    all_to_all x0 -> x1, blocking collectives: none -> 10.3 us  [exchange(): lax.all_to_all(blocks, 'sub', split_axis=0, concat_axis=0, tiled=True, ax...]
    pallas_call x0 -> x1, Pallas kernels: none -> 2.57 us  [outgoing_beams(): pl.pallas_call(functools.partial(beam_kernel, count), out_shape=jax.Shape...]
    gather x1 -> x0, local copies, waits for them, and re-layouts: 1.76 us -> none  [shards(): outgoing = beams.at[:, flat_ids].get(mode='promise_in_bounds')]
    squeeze x0 -> x1, other arithmetic: none -> 1.24 us  [shards(): spectra = spectra[0]]
    reduce_sum x3 -> x2, other arithmetic: 1.29 us -> 0.09 us  [the longest x1 0.08 us: energy_parts(): energy = jnp.sum(real * real + imag * imag, axis=1)]
    another operation x2 -> x1, other arithmetic: 4.33 us -> 4.2 us
  transfers between devices with their start and end apart: 3 -> 2, of which waited for: 3 -> 1; matrix products, arithmetic and copies ran while one was open for 7% -> 5% of each run, Pallas kernels for 0% -> 0%
where the time goes in v4:
time: 104 us; the launch traced here: 103 us
  waiting for transfers between devices  41.8 us (40%)
  starting transfers between devices  37 us (36%)
  blocking collectives  10.3 us (10%)
  other arithmetic  6.31 us (6%)
  Pallas kernels  5.68 us (5%)
  local copies, waits for them, and re-layouts  1.35 us (1%)
    all_to_all x2, waiting for transfers between devices, exchange(): lax.all_to_all(blocks, 'sub', split_axis=0, concat_axis=0, tiled=True, ax...  41.8 us
    all_to_all x2, starting transfers between devices, exchange(): lax.all_to_all(blocks, 'sub', split_axis=0, concat_axis=0, tiled=True, ax...  37 us
    all_to_all x1, blocking collectives, exchange(): lax.all_to_all(blocks, 'sub', split_axis=0, concat_axis=0, tiled=True, ax...  10.3 us
    another operation x1, other arithmetic  4.2 us
    pallas_call x1, Pallas kernels, pair_powers(): pl.pallas_call(functools.partial(pair_kernel, bins), out_shape=jax.ShapeD...  3.11 us
    pallas_call x1, Pallas kernels, outgoing_beams(): pl.pallas_call(functools.partial(beam_kernel, count), out_shape=jax.Shape...  2.57 us
  transfers between devices with their start and end apart: 2, of which 1 were waited for; matrix products, arithmetic and copies ran while one was open for 5% of the time, Pallas kernels for 0%

profile of v4, /device:TPU:6, one launch (start us, length us, event | category | flops | bytes accessed | tf_op | source)
XLA Modules:
  0.0 103.2 jit_solution(1191778556315364386)
XLA Ops:
  0.0 1.2 %copy_bitcast_fusion = (bf16[64,16,256]{2,0,1:T(8,128)(2,1)S(1)}, f32[64,16,256]{2,0,1:T(8,128)S(1)}) fusion(bf16[1,64,16,256]{3,2,1,0:T(8,128)(2,1)} %param.7), kind=kLoop, calls=%fused_computation.13 | loop fusion | flops 262144 | bytes 2097152 | tf_op jit(solution)/shard_map/squeeze | solution.py:186
  1.2 0.0 copy-start.2
  1.3 0.0 copy-start.3
  1.3 0.0 copy-start.4
  1.3 0.0 copy-start
  1.3 0.1 fusion.7
  1.4 10.3 %all_to_all.15 = f32[8,8,128]{2,1,0:T(8,128)S(1)} all-to-all(f32[8,8,128]{2,1,0:T(8,128)S(1)} %bitcast.18), channel_id=1, replica_groups={{34,35,32,33,38,39,36,37},{42,43,40,41,46,47,44,45},{50,51,48,49,54,55,..., dimensions={0} | all-to-all | bytes 65536 | tf_op jit(solution)/shard_map/all_to_all | solution.py:180
  11.7 0.0 copy-done.2
  11.7 0.0 copy-done.3
  11.7 0.0 copy-done.4
  11.7 0.0 copy-done
  11.7 0.1 fusion.13
  11.8 0.1 slice.41
  11.9 0.1 copy.20
  12.0 0.1 slice.43
  12.1 0.1 copy.21
  12.2 0.7 broadcast_in_dim.2
  12.9 21.1 %all-to-all-start.1 = ((bf16[64,8,128]{2,1,0:T(8,128)(2,1)}), bf16[64,8,128]{2,1,0:T(8,128)(2,1)S(1)}, u32[]{:S(2)}, u32[]{:S(2)}) async-start(bf16[64,8,128]{2,1,0:T(8,128)(2,1)} %broadcast_in_dim.2), calls=%async_computation.1 | async-start | bytes 262144 | tf_op jit(solution)/shard_map/all_to_all | solution.py:180
  33.9 0.1 fusion.8
  34.0 0.1 multiply_add_fusion
  34.1 0.1 copy.22
  34.2 4.2 %fusion.5 = (bf16[16,128,64]{2,1,0:T(8,128)(2,1)S(1)}, bf16[16,128,64]{2,1,0:T(8,128)(2,1)S(1)}, bf16[16,128,64]{2,1,0:T(8,128)(2,1)S(1)}) fusion(f32[128,64]{1,0:T(8,128)S(1)} %multiply_add_fusion, f32[16]{0:T(128)S(1)} %broadcast_multiply_fusion), kind=kLoop, calls=%fused_computation.7 | loop fusion | flops 917504 | bytes 819264 | tf_op jit(solution)/shard_map/convert.5
  38.5 0.6 maximum_maximum_fusion.matrix_ref
  39.0 0.0 all-to-all-done.1.code_ref
  39.1 2.6 %shard_map.73 = bf16[64,64,128]{2,1,0:T(8,128)(2,1)} custom-call(s32[64,4]{1,0:T(8,128)S(1)} %bitcast.17, bf16[64,8,128]{2,1,0:T(8,128)(2,1)S(1)} %all-to-all-done.1.code_ref, bf16[16,64,256]{2,1,0:T(8,128)(2,1)S(1)} %bitcast.16, bf16[16,256,128]{2,1,0:T(8,128)(2,1)S(1)} %maximum_maximum_fusion.matrix_ref), custom_call_target="tpu_custom_call" | custom-call | flops 67108864 | bytes 1572864 | tf_op jit(solution)/shard_map/pallas_call | solution.py:90
  41.6 0.0 copy-start.1
  41.6 15.9 %all-to-all-start.2 = ((bf16[64,64,128]{2,1,0:T(8,128)(2,1)}), bf16[64,64,128]{2,1,0:T(8,128)(2,1)S(1)}, u32[]{:S(2)}, u32[]{:S(2)}) async-start(bf16[64,64,128]{2,1,0:T(8,128)(2,1)} %shard_map.73), calls=%async_computation.2 | async-start | bytes 2097152 | tf_op jit(solution)/shard_map/all_to_all | solution.py:180
  57.6 0.0 copy-done.1
  57.6 0.1 copy.23.slots_ref
  58.4 41.8 %all-to-all-done.2.held_ref = bf16[64,64,128]{2,1,0:T(8,128)(2,1)S(1)} async-done(((bf16[64,64,128]{2,1,0:T(8,128)(2,1)}), bf16[64,64,128]{2,1,0:T(8,128)(2,1)S(1)}, u32[]{:S(2)}, u32[]{:S(2)}) %all-to-all-start.2) | async-done | bytes 1048608 | tf_op jit(solution)/shard_map/all_to_all | solution.py:180
  100.1 3.1 %shard_map.74 = f32[6,64,64]{2,1,0:T(8,128)} custom-call(s32[6,2]{1,0:T(8,128)S(1)} %copy.23.slots_ref, s32[1]{0:T(128)S(6)} %copy.27.count_ref, bf16[64,64,128]{2,1,0:T(8,128)(2,1)S(1)} %all-to-all-done.2.held_ref), custom_call_target="tpu_custom_call" | custom-call | flops 402653184 | bytes 1048576 | tf_op jit(solution)/shard_map/pallas_call | solution.py:153
  (6 shorter events, 0.0 us)
Async XLA Ops:
  1.2 10.4 %copy-start.2 = (f32[2,128]{1,0:T(2,128)S(1)}, f32[2,128]{1,0:T(2,128)}, u32[]{:S(2)}) copy-start(f32[2,128]{1,0:T(2,128)} %param.9) | copy-start | bytes 3076
  1.3 10.4 %copy-start.3 = (s32[64]{0:T(128)S(1)}, s32[64]{0:T(128)}, u32[]{:S(2)}) copy-start(s32[64]{0:T(128)} %param.10) | copy-start | bytes 772
  1.3 10.4 %copy-start.4 = (f32[16]{0:T(128)S(1)}, f32[16]{0:T(128)}, u32[]{:S(2)}) copy-start(f32[16]{0:T(128)} %param.8) | copy-start | bytes 196
  1.3 10.5 %copy-start = (s32[64,4]{0,1:T(4,128)S(1)}, s32[64,4]{0,1:T(4,128)}, u32[]{:S(2)}) copy-start(s32[64,4]{0,1:T(4,128)} %param.11) | copy-start | bytes 3076
  12.9 26.2 %all-to-all-start.1 = ((bf16[64,8,128]{2,1,0:T(8,128)(2,1)}), bf16[64,8,128]{2,1,0:T(8,128)(2,1)S(1)}, u32[]{:S(2)}, u32[]{:S(2)}) async-start(bf16[64,8,128]{2,1,0:T(8,128)(2,1)} %broadcast_in_dim.2), calls=%async_computation.1 | async-start | bytes 262144 | tf_op jit(solution)/shard_map/all_to_all | solution.py:180
  41.6 16.0 %copy-start.1 = (s32[1,6,2]{1,2,0:T(2,128)S(1)}, s32[1,6,2]{1,2,0:T(2,128)}, u32[]{:S(2)}) copy-start(s32[1,6,2]{1,2,0:T(2,128)} %param.12) | copy-start | bytes 148
  41.6 58.5 %all-to-all-start.2 = ((bf16[64,64,128]{2,1,0:T(8,128)(2,1)}), bf16[64,64,128]{2,1,0:T(8,128)(2,1)S(1)}, u32[]{:S(2)}, u32[]{:S(2)}) async-start(bf16[64,64,128]{2,1,0:T(8,128)(2,1)} %shard_map.73), calls=%async_computation.2 | async-start | bytes 2097152 | tf_op jit(solution)/shard_map/all_to_all | solution.py:180

commit v5 on v4

--- a/solution.py
+++ b/solution.py
@@ -10,35 +10,72 @@
 from jax.sharding import PartitionSpec as P
 
 COLUMNS = 4
-NEAR = 8
+DEEP = 2
 FIRST = (8, 2)
 
 slow_step = 0.04
 eps = 1e-06
 
 
+def steering_kernel(freqs_ref, offsets_ref, grid_ref, matrix_ref, delay):
+    stations, beams = delay.shape
+    block = 32
+    factor = stations ** (-0.5)
+    quarter = (lax.broadcasted_iota(jnp.int32, (block, beams), 1) >= beams // 2).astype(jnp.int32)
+    grid = jnp.concatenate([grid_ref[...], grid_ref[...]], axis=1)
+    slow_x = ((grid & 15).astype(jnp.float32) - 7.5) * slow_step
+    slow_y = ((grid >> 4).astype(jnp.float32) - 7.5) * slow_step
+    east = jnp.swapaxes(jnp.broadcast_to(offsets_ref[0:1, :], (beams, stations)), 0, 1)
+    north = jnp.swapaxes(jnp.broadcast_to(offsets_ref[1:2, :], (beams, stations)), 0, 1)
+    delay[...] = slow_x * east + slow_y * north
+
+    def one_bin(n, carry):
+        for row in range(0, stations, block):
+            phase = (2.0 * math.pi * freqs_ref[n]) * delay[row : row + block, :]
+            turns = jnp.floor(phase * (2.0 / math.pi) + 0.5)
+            rest = phase - turns * 1.5703125
+            rest = rest - turns * 4.837512969970703125e-4
+            rest = rest - turns * 7.54978995489188216e-8
+            square = rest * rest
+            sine = (-1.9515295891e-4 * square + 8.3321608736e-3) * square - 1.6666654611e-1
+            sine = sine * square * rest + rest
+            cosine = (2.443315711809948e-5 * square - 1.388731625493765e-3) * square
+            cosine = (cosine + 4.166664568298827e-2) * square * square - 0.5 * square + 1.0
+            which = turns.astype(jnp.int32) + quarter
+            odd = (which & 1) == 1
+            upper = jnp.where(odd, sine, cosine) * jnp.where(((which + 1) & 2) == 0, factor, -factor)
+            lower = jnp.where(odd, cosine, sine) * jnp.where((which & 2) == 0, factor, -factor)
+            matrix_ref[n, row : row + block, :] = upper.astype(jnp.bfloat16)
+            matrix_ref[n, stations + row : stations + row + block, :] = lower.astype(jnp.bfloat16)
+        return carry
+
+    lax.fori_loop(0, matrix_ref.shape[0], one_bin, 0)
+
+
 def steering(bin_freqs, station_offsets, beam_grid):
-    slow_x = ((beam_grid % 16).astype(jnp.float32) - 7.5) * slow_step
-    slow_y = ((beam_grid // 16).astype(jnp.float32) - 7.5) * slow_step
-    delay = (
-        slow_x[:, None] * station_offsets[0][None, :]
-        + slow_y[:, None] * station_offsets[1][None, :]
-    )
-    phase = 2.0 * math.pi * bin_freqs[:, None, None] * delay[None, :, :]
-    factor = station_offsets.shape[1] ** (-0.5)
-    cosine = jnp.swapaxes(jnp.cos(phase), 1, 2) * factor
-    sine = jnp.swapaxes(jnp.sin(phase), 1, 2) * factor
-    upper = jnp.concatenate([cosine, -sine], axis=2)
-    lower = jnp.concatenate([sine, cosine], axis=2)
-    return jnp.concatenate([upper, lower], axis=1).astype(jnp.bfloat16)
-
-
-def energy_parts(spectra, near):
-    subarrays, _, width = spectra.shape
+    bins, stations, beams = bin_freqs.shape[0], station_offsets.shape[1], 2 * beam_grid.shape[0]
+    smem = pl.BlockSpec(memory_space=pltpu.SMEM)
+    vmem = pl.BlockSpec(memory_space=pltpu.VMEM)
+    return pl.pallas_call(
+        steering_kernel,
+        out_shape=jax.ShapeDtypeStruct((bins, 2 * stations, beams), jnp.bfloat16),
+        in_specs=[smem, vmem, vmem],
+        out_specs=vmem,
+        scratch_shapes=[pltpu.VMEM((stations, beams), jnp.float32)],
+        compiler_params=pltpu.CompilerParams(vmem_limit_bytes=16 * 1024 * 1024),
+        cost_estimate=pl.CostEstimate(
+            flops=30 * bins * stations * beams,
+            bytes_accessed=4 * bins * stations * beams,
+            transcendentals=0,
+        ),
+    )(bin_freqs, station_offsets, beam_grid[None])
+
+
+def energies(spectra):
+    half = spectra.shape[2] // 2
     values = spectra.astype(jnp.float32)
-    real, imag = values[:, :, : width // 2], values[:, :, width // 2 :]
-    energy = jnp.sum(real * real + imag * imag, axis=1)
-    return energy.reshape(near, subarrays // near, width // 2)
+    real, imag = values[:, :, :half], values[:, :, half:]
+    return jnp.sum(real * real + imag * imag, axis=1)
 
 
 def encode(energy):
@@ -50,9 +87,9 @@
     return jnp.sqrt(jnp.sqrt(code.astype(jnp.float32))) * 256.0
 
 
-def beam_kernel(count, ids_ref, code_ref, spectra_ref, matrix_ref, out_ref, made, turned, chunk, sems):
+def beam_kernel(count, order, ids_ref, code_ref, spectra_ref, matrix_ref, out_ref, made, turned, chunk, sems):
     bins, subarrays, width = spectra_ref.shape
-    held = ids_ref.shape[1]
+    held = ids_ref.shape[0]
     steps, per_step = chunk.shape[0], chunk.shape[1]
     groups = decode(code_ref[...]).reshape(-1, subarrays, width // 2)
     scale = lax.rsqrt(jnp.sum(groups, axis=0) / count + eps)
@@ -68,7 +105,7 @@
         for own in range(per_step):
             for h in range(held):
                 chunk[step, own, h * bins : (h + 1) * bins] = turned[
-                    ids_ref[step * per_step + own, h]
+                    ids_ref[h, order[step * per_step + own]]
                 ]
         copies.append(
             pltpu.make_async_copy(
@@ -80,15 +117,15 @@
         copy.wait()
 
 
-def outgoing_beams(ids, code, spectra, matrix, count):
+def outgoing_beams(ids, order, code, spectra, matrix, count):
     bins, subarrays, width = spectra.shape
-    owners, held = ids.shape
+    held, owners = ids.shape
     beams = matrix.shape[2]
     steps = 8
     smem = pl.BlockSpec(memory_space=pltpu.SMEM)
     vmem = pl.BlockSpec(memory_space=pltpu.VMEM)
     return pl.pallas_call(
-        functools.partial(beam_kernel, count),
+        functools.partial(beam_kernel, count, order),
         out_shape=jax.ShapeDtypeStruct((owners, held * bins, beams), jnp.bfloat16),
         in_specs=[smem, vmem, vmem, vmem],
         out_specs=pl.BlockSpec(memory_space=pl.ANY),
@@ -138,8 +175,8 @@
     picked[2] = most[:, width : width + half] + most[:, width + half :]
     copies = []
     for p in range(power_ref.shape[0]):
-        row = pl.multiple_of(slots_ref[p, 0] * half, half)
-        power = picked[slots_ref[p, 1] - 1, pl.ds(row, half), :] / (bins * records)
+        row = pl.multiple_of(slots_ref[0, p] * half, half)
+        power = picked[slots_ref[1, p] - 1, pl.ds(row, half), :] / (bins * records)
         made[p] = jnp.where(p < count_ref[0], power, 0.0)
         copies.append(pltpu.make_async_copy(made.at[p], power_ref.at[p], sems.at[p]))
         copies[-1].start()
@@ -152,7 +189,7 @@
     half = width // 2
     return pl.pallas_call(
         functools.partial(pair_kernel, bins),
-        out_shape=jax.ShapeDtypeStruct((slots.shape[0], half, half), jnp.float32),
+        out_shape=jax.ShapeDtypeStruct((slots.shape[1], half, half), jnp.float32),
         in_specs=[
             pl.BlockSpec(memory_space=pltpu.SMEM),
             pl.BlockSpec(memory_space=pltpu.SMEM),
@@ -164,8 +201,8 @@
             pltpu.VMEM((3 * half, 2 * width), jnp.float32),
             pltpu.VMEM((half, width), jnp.float32),
             pltpu.VMEM((3, 3 * half, half), jnp.float32),
-            pltpu.VMEM((slots.shape[0], half, half), jnp.float32),
-            pltpu.SemaphoreType.DMA((slots.shape[0],)),
+            pltpu.VMEM((slots.shape[1], half, half), jnp.float32),
+            pltpu.SemaphoreType.DMA((slots.shape[1],)),
         ],
         compiler_params=pltpu.CompilerParams(vmem_limit_bytes=32 * 1024 * 1024),
         cost_estimate=pl.CostEstimate(
@@ -187,22 +224,25 @@
     bins = spectra.shape[1]
     records = lax.axis_size("sub")
     grid = np.arange(records).reshape(-1, COLUMNS)
-    order = np.roll(grid, (-FIRST[0], -FIRST[1]), (0, 1)).reshape(-1)
-    wide = [order.tolist()]
-    near = order.reshape(-1, NEAR).tolist()
-    parts = exchange(energy_parts(spectra, NEAR), near)
-    group = jnp.sum(parts, axis=0)
-    group, spectra, bin_freqs, station_offsets, beam_grid, owner_subarrays = lax.optimization_barrier(
-        (group, spectra, bin_freqs, station_offsets, beam_grid, owner_subarrays)
+    order = np.roll(grid, (-FIRST[0], -FIRST[1]), (0, 1))
+    wide = [order.reshape(-1).tolist()]
+    near = order.reshape(-1, DEEP * COLUMNS).tolist()
+    along = order.T.tolist()
+    energy = energies(spectra)
+    parts = energy.reshape(DEEP, 1, -1, energy.shape[1])
+    parts = jnp.broadcast_to(parts, (DEEP, COLUMNS, *parts.shape[2:]))
+    parts = exchange(parts.reshape(-1, *parts.shape[2:]), near)
+    code = encode(jnp.sum(parts, axis=0))
+    code = jnp.broadcast_to(code[None], (order.shape[0], *code.shape))
+    code, bin_freqs, station_offsets, beam_grid, owner_subarrays = lax.optimization_barrier(
+        (code, bin_freqs, station_offsets, beam_grid, owner_subarrays)
     )
-    code = encode(group)
-    code = exchange(jnp.broadcast_to(code[None], (records, *code.shape)), wide)
+    code = exchange(code, along)
     matrix = steering(bin_freqs, station_offsets, beam_grid)
-    owners = owner_subarrays.reshape(-1, COLUMNS, owner_subarrays.shape[1])
-    owners = jnp.roll(owners, (-FIRST[0], -FIRST[1]), (0, 1)).reshape(owner_subarrays.shape)
-    outgoing = outgoing_beams(owners, code, jnp.swapaxes(spectra, 0, 1), matrix, records * bins)
+    spectra = jnp.swapaxes(spectra, 0, 1)
+    outgoing = outgoing_beams(owner_subarrays.T, wide[0], code, spectra, matrix, records * bins)
     held = exchange(outgoing, wide)
-    return pair_powers(pair_slots[0], pair_count, held, bins)
+    return pair_powers(pair_slots[0].T, pair_count, held, bins)
 
 
 def solution(mesh):

time: 104 us -> 100 us (0.962)
  other arithmetic: 6.31 us -> 1.33 us
  starting transfers between devices: 37 us -> 33.1 us
  waiting for transfers between devices: 41.8 us -> 45.2 us
  Pallas kernels: 5.68 us -> 7.4 us
    another operation x1 -> x0, other arithmetic: 4.2 us -> none
    all_to_all x2, starting transfers between devices: 37 us -> 33.1 us  [exchange(): lax.all_to_all(blocks, 'sub', split_axis=0, concat_axis=0, tiled=True, ax...]
    all_to_all x2, waiting for transfers between devices: 41.8 us -> 45.2 us  [exchange(): lax.all_to_all(blocks, 'sub', split_axis=0, concat_axis=0, tiled=True, ax...]
    pallas_call x1 -> x2, Pallas kernels: 2.57 us -> 4.35 us  [the longest x1 2.28 us: steering(): pl.pallas_call(steering_kernel, out_shape=jax.ShapeDtypeStruct((bins, 2 *...]
    squeeze x1 -> x0, other arithmetic: 1.24 us -> none  [shards(): spectra = spectra[0]]
    transpose x0 -> x1, other arithmetic: none -> 1.24 us  [shards(): spectra = jnp.swapaxes(spectra, 0, 1)]
  transfers between devices with their start and end apart: 2 -> 2, of which waited for: 1 -> 2; matrix products, arithmetic and copies ran while one was open for 5% -> 0% of each run, Pallas kernels for 0% -> 2%
where the time goes in v5:
time: 100 us; the launch traced here: 99.9 us
  waiting for transfers between devices  45.2 us (45%)
  starting transfers between devices  33.1 us (33%)
  blocking collectives  10.8 us (11%)
  Pallas kernels  7.4 us (7%)
  local copies, waits for them, and re-layouts  1.36 us (1%)
  other arithmetic  1.33 us (1%)
    all_to_all x2, waiting for transfers between devices, exchange(): lax.all_to_all(blocks, 'sub', split_axis=0, concat_axis=0, tiled=True, ax...  45.2 us
    all_to_all x2, starting transfers between devices, exchange(): lax.all_to_all(blocks, 'sub', split_axis=0, concat_axis=0, tiled=True, ax...  33.1 us
    all_to_all x1, blocking collectives, exchange(): lax.all_to_all(blocks, 'sub', split_axis=0, concat_axis=0, tiled=True, ax...  10.8 us
    pallas_call x1, Pallas kernels, pair_powers(): pl.pallas_call(functools.partial(pair_kernel, bins), out_shape=jax.ShapeD...  3.06 us
    pallas_call x1, Pallas kernels, steering(): pl.pallas_call(steering_kernel, out_shape=jax.ShapeDtypeStruct((bins, 2 *...  2.28 us
    pallas_call x1, Pallas kernels, outgoing_beams(): pl.pallas_call(functools.partial(beam_kernel, count, order), out_shape=ja...  2.07 us
  transfers between devices with their start and end apart: 2, of which 2 were waited for; matrix products, arithmetic and copies ran while one was open for 0% of the time, Pallas kernels for 2%

profile of v5, /device:TPU:6, one launch (start us, length us, event | category | flops | bytes accessed | tf_op | source)
XLA Modules:
  0.0 99.9 jit_solution(5829124242538773928)
XLA Ops:
  0.0 1.2 %copy_bitcast_fusion = (bf16[16,64,256]{2,1,0:T(8,128)(2,1)S(1)}, f32[64,16,256]{2,0,1:T(8,128)S(1)}) fusion(bf16[1,64,16,256]{3,2,1,0:T(8,128)(2,1)} %param.7), kind=kLoop, calls=%fused_computation.5 | loop fusion | flops 262144 | bytes 2097152 | tf_op jit(solution)/shard_map/transpose | solution.py:242
  1.2 0.1 fusion.1
  1.3 10.8 %all_to_all.15 = f32[8,32,128]{2,1,0:T(8,128)S(1)} all-to-all(f32[8,32,128]{2,1,0:T(8,128)S(1)} %bitcast.15), channel_id=1, replica_groups={{34,35,32,33,38,39,36,37},{42,43,40,41,46,47,44,45},{50,51,48,49,54,55,..., dimensions={0} | all-to-all | bytes 262144 | tf_op jit(solution)/shard_map/all_to_all | solution.py:217
  12.2 0.7 broadcast_in_dim.18
  12.9 0.0 copy-start.3
  12.9 17.6 %all-to-all-start.1 = ((bf16[16,32,128]{2,1,0:T(8,128)(2,1)}), bf16[16,32,128]{2,1,0:T(8,128)(2,1)S(1)}, u32[]{:S(2)}, u32[]{:S(2)}) async-start(bf16[16,32,128]{2,1,0:T(8,128)(2,1)} %broadcast_in_dim.18), calls=%async_computation.1 | async-start | bytes 262144 | tf_op jit(solution)/shard_map/all_to_all | solution.py:217
  30.5 0.0 copy-start.1
  30.5 0.0 copy-start.2
  30.5 0.0 copy-done.3
  30.5 0.6 copy-done.1
  31.2 0.0 copy-done.2
  31.2 2.3 %shard_map.73.matrix_ref = bf16[16,256,128]{2,1,0:T(8,128)(2,1)S(1)} custom-call(f32[16]{0:T(128)S(1)} %copy-done.2, f32[2,128]{1,0:T(2,128)S(1)} %copy-done.1, s32[1,64]{1,0:T(1,128)S(1)} %bitcast.13), custom_call_target="tpu_custom_call" | custom-call | flops 7864320 | bytes 1048576 | tf_op jit(solution)/shard_map/pallas_call | solution.py:59
  33.5 0.0 copy-start
  33.5 2.4 %all-to-all-done.1.code_ref = bf16[16,32,128]{2,1,0:T(8,128)(2,1)S(1)} async-done(((bf16[16,32,128]{2,1,0:T(8,128)(2,1)}), bf16[16,32,128]{2,1,0:T(8,128)(2,1)S(1)}, u32[]{:S(2)}, u32[]{:S(2)}) %all-to-all-start.1) | async-done | bytes 131104 | tf_op jit(solution)/shard_map/all_to_all | solution.py:217
  35.9 0.0 copy-done
  35.9 2.1 %shard_map.74 = bf16[64,64,128]{2,1,0:T(8,128)(2,1)} custom-call(s32[4,64]{1,0:T(4,128)S(1)} %bitcast.12, bf16[16,32,128]{2,1,0:T(8,128)(2,1)S(1)} %all-to-all-done.1.code_ref, bf16[16,64,256]{2,1,0:T(8,128)(2,1)S(1)} %get-tuple-element.15.spectra_ref, bf16[16,256,128]{2,1,0:T(8,128)(2,1)S(1)} %shard_map.73.matrix_ref), custom_call_target="tpu_custom_call" | custom-call | flops 67108864 | bytes 1572864 | tf_op jit(solution)/shard_map/pallas_call | solution.py:127
  37.9 15.5 %all-to-all-start.2 = ((bf16[64,64,128]{2,1,0:T(8,128)(2,1)}), bf16[64,64,128]{2,1,0:T(8,128)(2,1)S(1)}, u32[]{:S(2)}, u32[]{:S(2)}) async-start(bf16[64,64,128]{2,1,0:T(8,128)(2,1)} %shard_map.74), calls=%async_computation.2 | async-start | bytes 2097152 | tf_op jit(solution)/shard_map/all_to_all | solution.py:217
  54.1 0.0 copy-start.4
  54.1 42.8 %all-to-all-done.2.held_ref = bf16[64,64,128]{2,1,0:T(8,128)(2,1)S(1)} async-done(((bf16[64,64,128]{2,1,0:T(8,128)(2,1)}), bf16[64,64,128]{2,1,0:T(8,128)(2,1)S(1)}, u32[]{:S(2)}, u32[]{:S(2)}) %all-to-all-start.2) | async-done | bytes 1048608 | tf_op jit(solution)/shard_map/all_to_all | solution.py:217
  96.9 0.0 copy-done.4
  96.9 3.1 %shard_map.75 = f32[6,64,64]{2,1,0:T(8,128)} custom-call(s32[2,6]{1,0:T(2,128)S(1)} %bitcast.14, s32[1]{0:T(128)S(6)} %copy.12.count_ref, bf16[64,64,128]{2,1,0:T(8,128)(2,1)S(1)} %all-to-all-done.2.held_ref), custom_call_target="tpu_custom_call" | custom-call | flops 402653184 | bytes 1048576 | tf_op jit(solution)/shard_map/pallas_call | solution.py:190
  (3 shorter events, 0.0 us)
Async XLA Ops:
  12.9 17.7 %copy-start.3 = (s32[64]{0:T(128)S(1)}, s32[64]{0:T(128)}, u32[]{:S(2)}) copy-start(s32[64]{0:T(128)} %param.10) | copy-start | bytes 772
  12.9 23.0 %all-to-all-start.1 = ((bf16[16,32,128]{2,1,0:T(8,128)(2,1)}), bf16[16,32,128]{2,1,0:T(8,128)(2,1)S(1)}, u32[]{:S(2)}, u32[]{:S(2)}) async-start(bf16[16,32,128]{2,1,0:T(8,128)(2,1)} %broadcast_in_dim.18), calls=%async_computation.1 | async-start | bytes 262144 | tf_op jit(solution)/shard_map/all_to_all | solution.py:217
  30.5 0.7 copy-start.1
  30.5 0.7 copy-start.2
  33.5 2.4 %copy-start = (s32[64,4]{0,1:T(4,128)S(1)}, s32[64,4]{0,1:T(4,128)}, u32[]{:S(2)}) copy-start(s32[64,4]{0,1:T(4,128)} %param.11) | copy-start | bytes 3076
  37.9 58.9 %all-to-all-start.2 = ((bf16[64,64,128]{2,1,0:T(8,128)(2,1)}), bf16[64,64,128]{2,1,0:T(8,128)(2,1)S(1)}, u32[]{:S(2)}, u32[]{:S(2)}) async-start(bf16[64,64,128]{2,1,0:T(8,128)(2,1)} %shard_map.74), calls=%async_computation.2 | async-start | bytes 2097152 | tf_op jit(solution)/shard_map/all_to_all | solution.py:217
  54.1 42.8 %copy-start.4 = (s32[1,6,2]{1,2,0:T(2,128)S(1)}, s32[1,6,2]{1,2,0:T(2,128)}, u32[]{:S(2)}) copy-start(s32[1,6,2]{1,2,0:T(2,128)} %param.12) | copy-start | bytes 148

commit v6 on v5

--- a/solution.py
+++ b/solution.py
@@ -12,6 +12,7 @@
 COLUMNS = 4
 DEEP = 2
 FIRST = (8, 2)
+ALONG = 10
 
 slow_step = 0.04
 eps = 1e-06
@@ -87,7 +88,11 @@
     return jnp.sqrt(jnp.sqrt(code.astype(jnp.float32))) * 256.0
 
 
-def beam_kernel(count, order, ids_ref, code_ref, spectra_ref, matrix_ref, out_ref, made, turned, chunk, sems):
+def beam_kernel(
+    count, order, ids_any, code_ref, spectra_ref, matrix_ref, out_ref, ids_ref, made, turned, chunk, sems, ids_sem
+):
+    ids_copy = pltpu.make_async_copy(ids_any, ids_ref, ids_sem)
+    ids_copy.start()
     bins, subarrays, width = spectra_ref.shape
     held = ids_ref.shape[0]
     steps, per_step = chunk.shape[0], chunk.shape[1]
@@ -100,6 +105,7 @@
             white, matrix_ref[n], preferred_element_type=jnp.float32
         ).astype(jnp.bfloat16)
     turned[...] = jnp.swapaxes(made[...], 0, 1)
+    ids_copy.wait()
     copies = []
     for step in range(steps):
         for own in range(per_step):
@@ -122,18 +128,20 @@
     held, owners = ids.shape
     beams = matrix.shape[2]
     steps = 8
-    smem = pl.BlockSpec(memory_space=pltpu.SMEM)
+    anywhere = pl.BlockSpec(memory_space=pl.ANY)
     vmem = pl.BlockSpec(memory_space=pltpu.VMEM)
     return pl.pallas_call(
         functools.partial(beam_kernel, count, order),
         out_shape=jax.ShapeDtypeStruct((owners, held * bins, beams), jnp.bfloat16),
-        in_specs=[smem, vmem, vmem, vmem],
-        out_specs=pl.BlockSpec(memory_space=pl.ANY),
+        in_specs=[anywhere, vmem, vmem, vmem],
+        out_specs=anywhere,
         scratch_shapes=[
+            pltpu.SMEM(ids.shape, jnp.int32),
             pltpu.VMEM((bins, subarrays, beams), jnp.bfloat16),
             pltpu.VMEM((subarrays, bins, beams), jnp.bfloat16),
             pltpu.VMEM((steps, owners // steps, held * bins, beams), jnp.bfloat16),
             pltpu.SemaphoreType.DMA((steps,)),
+            pltpu.SemaphoreType.DMA,
         ],
         compiler_params=pltpu.CompilerParams(vmem_limit_bytes=32 * 1024 * 1024),
         cost_estimate=pl.CostEstimate(
@@ -144,16 +152,23 @@
     )(ids, code, spectra, matrix)
 
 
-def pair_kernel(bins, slots_ref, count_ref, held_ref, power_ref, turned_ref, most, rest, picked, made, sems):
+def pair_kernel(
+    bins, slots_any, count_any, held_ref, power_ref, slots_ref, count_ref, most, rest, picked, made, sems, slot_sems
+):
+    slot_copies = [
+        pltpu.make_async_copy(slots_any, slots_ref, slot_sems.at[0]),
+        pltpu.make_async_copy(count_any, count_ref, slot_sems.at[1]),
+    ]
+    for copy in slot_copies:
+        copy.start()
     records, _, width = held_ref.shape
     half = width // 2
-    for h in range(4):
-        turned_ref[h] = jnp.swapaxes(held_ref[:, h * bins : (h + 1) * bins, :], 0, 1)
+    turned = [
+        jnp.swapaxes(held_ref[:, h * bins : (h + 1) * bins, :], 0, 1) for h in range(4)
+    ]
     low = lax.broadcasted_iota(jnp.int32, (records, width), 1) < half
-    most[...] = jnp.zeros_like(most)
-    rest[...] = jnp.zeros_like(rest)
     for n in range(bins):
-        held = [turned_ref[h, n] for h in range(4)]
+        held = [turned[h][n] for h in range(4)]
         rolled = [pltpu.roll(x, half, 1) for x in held]
         real = jnp.concatenate([jnp.where(low, held[0], rolled[1]), held[2]], axis=1)
         imag = jnp.concatenate([jnp.where(low, rolled[0], held[1]), rolled[2]], axis=1)
@@ -165,14 +180,16 @@
         two = jnp.concatenate(second[1:], axis=1)
         dims = (((0,), (0,)), ((), ()))
         cross = lax.dot_general(first, two, dims, preferred_element_type=jnp.float32)
-        most[...] += cross * cross
+        most[...] = cross * cross if n == 0 else most[...] + cross * cross
         cross = lax.dot_general(
             first[:, :half], second[0], dims, preferred_element_type=jnp.float32
         )
-        rest[...] += cross * cross
+        rest[...] = cross * cross if n == 0 else rest[...] + cross * cross
     picked[0, :half] = rest[:, :half] + rest[:, half:]
     picked[1] = most[:, :half] + most[:, half:width]
     picked[2] = most[:, width : width + half] + most[:, width + half :]
+    for copy in slot_copies:
+        copy.wait()
     copies = []
     for p in range(power_ref.shape[0]):
         row = pl.multiple_of(slots_ref[0, p] * half, half)
@@ -191,18 +208,20 @@
         functools.partial(pair_kernel, bins),
         out_shape=jax.ShapeDtypeStruct((slots.shape[1], half, half), jnp.float32),
         in_specs=[
-            pl.BlockSpec(memory_space=pltpu.SMEM),
-            pl.BlockSpec(memory_space=pltpu.SMEM),
+            pl.BlockSpec(memory_space=pl.ANY),
+            pl.BlockSpec(memory_space=pl.ANY),
             pl.BlockSpec(memory_space=pltpu.VMEM),
         ],
         out_specs=pl.BlockSpec(memory_space=pl.ANY),
         scratch_shapes=[
-            pltpu.VMEM((4, bins, records, width), jnp.bfloat16),
+            pltpu.SMEM(slots.shape, jnp.int32),
+            pltpu.SMEM(count.shape, jnp.int32),
             pltpu.VMEM((3 * half, 2 * width), jnp.float32),
             pltpu.VMEM((half, width), jnp.float32),
             pltpu.VMEM((3, 3 * half, half), jnp.float32),
             pltpu.VMEM((slots.shape[1], half, half), jnp.float32),
             pltpu.SemaphoreType.DMA((slots.shape[1],)),
+            pltpu.SemaphoreType.DMA((2,)),
         ],
         compiler_params=pltpu.CompilerParams(vmem_limit_bytes=32 * 1024 * 1024),
         cost_estimate=pl.CostEstimate(
@@ -227,7 +246,7 @@
     order = np.roll(grid, (-FIRST[0], -FIRST[1]), (0, 1))
     wide = [order.reshape(-1).tolist()]
     near = order.reshape(-1, DEEP * COLUMNS).tolist()
-    along = order.T.tolist()
+    along = np.roll(grid, -ALONG, 0).T.tolist()
     energy = energies(spectra)
     parts = energy.reshape(DEEP, 1, -1, energy.shape[1])
     parts = jnp.broadcast_to(parts, (DEEP, COLUMNS, *parts.shape[2:]))

time: 100 us -> 98.7 us (0.987)
  starting transfers between devices: 33.1 us -> 31.4 us
    all_to_all x2, starting transfers between devices: 33.1 us -> 31.4 us  [exchange(): lax.all_to_all(blocks, 'sub', split_axis=0, concat_axis=0, tiled=True, ax...]
where the time goes in v6:
time: 98.7 us; the launch traced here: 98.3 us
  waiting for transfers between devices  45.8 us (46%)
  starting transfers between devices  31.4 us (32%)
  blocking collectives  10.8 us (11%)
  Pallas kernels  6.75 us (7%)
  local copies, waits for them, and re-layouts  1.36 us (1%)
  other arithmetic  1.33 us (1%)
    all_to_all x2, waiting for transfers between devices, exchange(): lax.all_to_all(blocks, 'sub', split_axis=0, concat_axis=0, tiled=True, ax...  45.8 us
    all_to_all x2, starting transfers between devices, exchange(): lax.all_to_all(blocks, 'sub', split_axis=0, concat_axis=0, tiled=True, ax...  31.4 us
    all_to_all x1, blocking collectives, exchange(): lax.all_to_all(blocks, 'sub', split_axis=0, concat_axis=0, tiled=True, ax...  10.8 us
    pallas_call x1, Pallas kernels, pair_powers(): pl.pallas_call(functools.partial(pair_kernel, bins), out_shape=jax.ShapeD...  2.83 us
    pallas_call x1, Pallas kernels, steering(): pl.pallas_call(steering_kernel, out_shape=jax.ShapeDtypeStruct((bins, 2 *...  2.28 us
  transfers between devices with their start and end apart: 2, of which 2 were waited for; matrix products, arithmetic and copies ran while one was open for 0% of the time, Pallas kernels for 2%

profile of v6, /device:TPU:6, one launch (start us, length us, event | category | flops | bytes accessed | tf_op | source)
XLA Modules:
  0.0 98.3 jit_solution(5729029587987467752)
XLA Ops:
  0.0 1.2 %copy_bitcast_fusion = (bf16[16,64,256]{2,1,0:T(8,128)(2,1)S(1)}, f32[64,16,256]{2,0,1:T(8,128)S(1)}) fusion(bf16[1,64,16,256]{3,2,1,0:T(8,128)(2,1)} %param.7), kind=kLoop, calls=%fused_computation.5 | loop fusion | flops 262144 | bytes 2097152 | tf_op jit(solution)/shard_map/transpose | solution.py:261
  1.2 0.1 fusion.1
  1.3 10.8 %all_to_all.15 = f32[8,32,128]{2,1,0:T(8,128)S(1)} all-to-all(f32[8,32,128]{2,1,0:T(8,128)S(1)} %bitcast.15), channel_id=1, replica_groups={{34,35,32,33,38,39,36,37},{42,43,40,41,46,47,44,45},{50,51,48,49,54,55,..., dimensions={0} | all-to-all | bytes 262144 | tf_op jit(solution)/shard_map/all_to_all | solution.py:236
  12.2 0.7 broadcast_in_dim.18
  12.9 0.0 copy-start.3
  12.9 15.8 %all-to-all-start.1 = ((bf16[16,32,128]{2,1,0:T(8,128)(2,1)}), bf16[16,32,128]{2,1,0:T(8,128)(2,1)S(1)}, u32[]{:S(2)}, u32[]{:S(2)}) async-start(bf16[16,32,128]{2,1,0:T(8,128)(2,1)} %broadcast_in_dim.18), calls=%async_computation.1 | async-start | bytes 262144 | tf_op jit(solution)/shard_map/all_to_all | solution.py:236
  28.7 0.0 copy-start.1
  28.7 0.0 copy-start.2
  28.7 0.0 copy-done.3
  28.7 0.6 copy-done.1
  29.4 0.0 copy-done.2
  29.4 2.3 %shard_map.73.matrix_ref = bf16[16,256,128]{2,1,0:T(8,128)(2,1)S(1)} custom-call(f32[16]{0:T(128)S(1)} %copy-done.2, f32[2,128]{1,0:T(2,128)S(1)} %copy-done.1, s32[1,64]{1,0:T(1,128)S(1)} %bitcast.13), custom_call_target="tpu_custom_call" | custom-call | flops 7864320 | bytes 1048576 | tf_op jit(solution)/shard_map/pallas_call | solution.py:60
  31.7 0.0 copy-start
  31.7 3.9 %all-to-all-done.1.code_ref = bf16[16,32,128]{2,1,0:T(8,128)(2,1)S(1)} async-done(((bf16[16,32,128]{2,1,0:T(8,128)(2,1)}), bf16[16,32,128]{2,1,0:T(8,128)(2,1)S(1)}, u32[]{:S(2)}, u32[]{:S(2)}) %all-to-all-start.1) | async-done | bytes 131104 | tf_op jit(solution)/shard_map/all_to_all | solution.py:236
  35.6 0.0 copy-done
  35.6 1.6 %shard_map.74 = bf16[64,64,128]{2,1,0:T(8,128)(2,1)} custom-call(s32[4,64]{1,0:T(4,128)S(1)} %bitcast.12, bf16[16,32,128]{2,1,0:T(8,128)(2,1)S(1)} %all-to-all-done.1.code_ref, bf16[16,64,256]{2,1,0:T(8,128)(2,1)S(1)} %get-tuple-element.15.spectra_ref, bf16[16,256,128]{2,1,0:T(8,128)(2,1)S(1)} %shard_map.73.matrix_ref), custom_call_target="tpu_custom_call" | custom-call | flops 67108864 | bytes 1572864 | tf_op jit(solution)/shard_map/pallas_call | solution.py:133
  37.3 15.6 %all-to-all-start.2 = ((bf16[64,64,128]{2,1,0:T(8,128)(2,1)}), bf16[64,64,128]{2,1,0:T(8,128)(2,1)S(1)}, u32[]{:S(2)}, u32[]{:S(2)}) async-start(bf16[64,64,128]{2,1,0:T(8,128)(2,1)} %shard_map.74), calls=%async_computation.2 | async-start | bytes 2097152 | tf_op jit(solution)/shard_map/all_to_all | solution.py:236
  53.5 0.0 copy-start.4
  53.5 41.9 %all-to-all-done.2.held_ref = bf16[64,64,128]{2,1,0:T(8,128)(2,1)S(1)} async-done(((bf16[64,64,128]{2,1,0:T(8,128)(2,1)}), bf16[64,64,128]{2,1,0:T(8,128)(2,1)S(1)}, u32[]{:S(2)}, u32[]{:S(2)}) %all-to-all-start.2) | async-done | bytes 1048608 | tf_op jit(solution)/shard_map/all_to_all | solution.py:236
  95.4 0.0 copy-done.4
  95.4 2.8 %shard_map.75 = f32[6,64,64]{2,1,0:T(8,128)} custom-call(s32[2,6]{1,0:T(2,128)S(1)} %bitcast.14, s32[1]{0:T(128)S(6)} %copy.12.count_any, bf16[64,64,128]{2,1,0:T(8,128)(2,1)S(1)} %all-to-all-done.2.held_ref), custom_call_target="tpu_custom_call" | custom-call | flops 402653184 | bytes 1048576 | tf_op jit(solution)/shard_map/pallas_call | solution.py:207
  (3 shorter events, 0.0 us)
Async XLA Ops:
  12.9 15.9 %copy-start.3 = (s32[64]{0:T(128)S(1)}, s32[64]{0:T(128)}, u32[]{:S(2)}) copy-start(s32[64]{0:T(128)} %param.10) | copy-start | bytes 772
  12.9 22.8 %all-to-all-start.1 = ((bf16[16,32,128]{2,1,0:T(8,128)(2,1)}), bf16[16,32,128]{2,1,0:T(8,128)(2,1)S(1)}, u32[]{:S(2)}, u32[]{:S(2)}) async-start(bf16[16,32,128]{2,1,0:T(8,128)(2,1)} %broadcast_in_dim.18), calls=%async_computation.1 | async-start | bytes 262144 | tf_op jit(solution)/shard_map/all_to_all | solution.py:236
  28.7 0.7 copy-start.1
  28.7 0.7 copy-start.2
  31.7 4.0 %copy-start = (s32[64,4]{0,1:T(4,128)S(1)}, s32[64,4]{0,1:T(4,128)}, u32[]{:S(2)}) copy-start(s32[64,4]{0,1:T(4,128)} %param.11) | copy-start | bytes 3076
  37.3 58.2 %all-to-all-start.2 = ((bf16[64,64,128]{2,1,0:T(8,128)(2,1)}), bf16[64,64,128]{2,1,0:T(8,128)(2,1)S(1)}, u32[]{:S(2)}, u32[]{:S(2)}) async-start(bf16[64,64,128]{2,1,0:T(8,128)(2,1)} %shard_map.74), calls=%async_computation.2 | async-start | bytes 2097152 | tf_op jit(solution)/shard_map/all_to_all | solution.py:236
  53.5 41.9 %copy-start.4 = (s32[1,6,2]{1,2,0:T(2,128)S(1)}, s32[1,6,2]{1,2,0:T(2,128)}, u32[]{:S(2)}) copy-start(s32[1,6,2]{1,2,0:T(2,128)} %param.12) | copy-start | bytes 148

commit v7 on v6

--- a/solution.py
+++ b/solution.py
@@ -153,7 +153,7 @@
 
 
 def pair_kernel(
-    bins, slots_any, count_any, held_ref, power_ref, slots_ref, count_ref, most, rest, picked, made, sems, slot_sems
+    bins, slots_any, count_any, held_ref, power_ref, slots_ref, count_ref, most, rest, picked, slot_sems
 ):
     slot_copies = [
         pltpu.make_async_copy(slots_any, slots_ref, slot_sems.at[0]),
@@ -190,15 +190,10 @@
     picked[2] = most[:, width : width + half] + most[:, width + half :]
     for copy in slot_copies:
         copy.wait()
-    copies = []
     for p in range(power_ref.shape[0]):
         row = pl.multiple_of(slots_ref[0, p] * half, half)
         power = picked[slots_ref[1, p] - 1, pl.ds(row, half), :] / (bins * records)
-        made[p] = jnp.where(p < count_ref[0], power, 0.0)
-        copies.append(pltpu.make_async_copy(made.at[p], power_ref.at[p], sems.at[p]))
-        copies[-1].start()
-    for copy in copies:
-        copy.wait()
+        power_ref[p] = jnp.where(p < count_ref[0], power, 0.0)
 
 
 def pair_powers(slots, count, held, bins):
@@ -212,15 +207,13 @@
             pl.BlockSpec(memory_space=pl.ANY),
             pl.BlockSpec(memory_space=pltpu.VMEM),
         ],
-        out_specs=pl.BlockSpec(memory_space=pl.ANY),
+        out_specs=pl.BlockSpec(memory_space=pltpu.VMEM),
         scratch_shapes=[
             pltpu.SMEM(slots.shape, jnp.int32),
             pltpu.SMEM(count.shape, jnp.int32),
             pltpu.VMEM((3 * half, 2 * width), jnp.float32),
             pltpu.VMEM((half, width), jnp.float32),
             pltpu.VMEM((3, 3 * half, half), jnp.float32),
-            pltpu.VMEM((slots.shape[1], half, half), jnp.float32),
-            pltpu.SemaphoreType.DMA((slots.shape[1],)),
             pltpu.SemaphoreType.DMA((2,)),
         ],
         compiler_params=pltpu.CompilerParams(vmem_limit_bytes=32 * 1024 * 1024),
@@ -245,7 +238,7 @@
     grid = np.arange(records).reshape(-1, COLUMNS)
     order = np.roll(grid, (-FIRST[0], -FIRST[1]), (0, 1))
     wide = [order.reshape(-1).tolist()]
-    near = order.reshape(-1, DEEP * COLUMNS).tolist()
+    near = np.roll(grid, -2, 1).reshape(-1, DEEP * COLUMNS).tolist()
     along = np.roll(grid, -ALONG, 0).T.tolist()
     energy = energies(spectra)
     parts = energy.reshape(DEEP, 1, -1, energy.shape[1])

time: 98.7 us -> 98.2 us (level)
  no operation moved by 1% of the time
where the time goes in v7:
time: 98.2 us; the launch traced here: 97.9 us
  waiting for transfers between devices  45.8 us (47%)
  starting transfers between devices  31.4 us (32%)
  blocking collectives  10.8 us (11%)
  Pallas kernels  6.33 us (6%)
  local copies, waits for them, and re-layouts  1.36 us (1%)
  other arithmetic  1.33 us (1%)
    all_to_all x2, waiting for transfers between devices, exchange(): lax.all_to_all(blocks, 'sub', split_axis=0, concat_axis=0, tiled=True, ax...  45.8 us
    all_to_all x2, starting transfers between devices, exchange(): lax.all_to_all(blocks, 'sub', split_axis=0, concat_axis=0, tiled=True, ax...  31.4 us
    all_to_all x1, blocking collectives, exchange(): lax.all_to_all(blocks, 'sub', split_axis=0, concat_axis=0, tiled=True, ax...  10.8 us
    pallas_call x1, Pallas kernels, pair_powers(): pl.pallas_call(functools.partial(pair_kernel, bins), out_shape=jax.ShapeD...  2.41 us
    pallas_call x1, Pallas kernels, steering(): pl.pallas_call(steering_kernel, out_shape=jax.ShapeDtypeStruct((bins, 2 *...  2.28 us
  transfers between devices with their start and end apart: 2, of which 2 were waited for; matrix products, arithmetic and copies ran while one was open for 0% of the time, Pallas kernels for 2%

profile of v7, /device:TPU:6, one launch (start us, length us, event | category | flops | bytes accessed | tf_op | source)
XLA Modules:
  0.0 97.9 jit_solution(4937553174015726488)
XLA Ops:
  0.0 1.2 %copy_bitcast_fusion = (bf16[16,64,256]{2,1,0:T(8,128)(2,1)S(1)}, f32[64,16,256]{2,0,1:T(8,128)S(1)}) fusion(bf16[1,64,16,256]{3,2,1,0:T(8,128)(2,1)} %param.7), kind=kLoop, calls=%fused_computation.5 | loop fusion | flops 262144 | bytes 2097152 | tf_op jit(solution)/shard_map/transpose | solution.py:254
  1.2 0.1 fusion.1
  1.3 10.8 %all_to_all.15 = f32[8,32,128]{2,1,0:T(8,128)S(1)} all-to-all(f32[8,32,128]{2,1,0:T(8,128)S(1)} %bitcast.15), channel_id=1, replica_groups={{2,3,0,1,6,7,4,5},{10,11,8,9,14,15,12,13},{18,19,16,17,22,23,20,21},{26..., dimensions={0} | all-to-all | bytes 262144 | tf_op jit(solution)/shard_map/all_to_all | solution.py:229
  12.2 0.7 broadcast_in_dim.18
  12.9 0.0 copy-start.3
  12.9 15.8 %all-to-all-start.1 = ((bf16[16,32,128]{2,1,0:T(8,128)(2,1)}), bf16[16,32,128]{2,1,0:T(8,128)(2,1)S(1)}, u32[]{:S(2)}, u32[]{:S(2)}) async-start(bf16[16,32,128]{2,1,0:T(8,128)(2,1)} %broadcast_in_dim.18), calls=%async_computation.1 | async-start | bytes 262144 | tf_op jit(solution)/shard_map/all_to_all | solution.py:229
  28.7 0.0 copy-start.1
  28.7 0.0 copy-start.2
  28.7 0.0 copy-done.3
  28.7 0.6 copy-done.1
  29.4 0.0 copy-done.2
  29.4 2.3 %shard_map.73.matrix_ref = bf16[16,256,128]{2,1,0:T(8,128)(2,1)S(1)} custom-call(f32[16]{0:T(128)S(1)} %copy-done.2, f32[2,128]{1,0:T(2,128)S(1)} %copy-done.1, s32[1,64]{1,0:T(1,128)S(1)} %bitcast.13), custom_call_target="tpu_custom_call" | custom-call | flops 7864320 | bytes 1048576 | tf_op jit(solution)/shard_map/pallas_call | solution.py:60
  31.7 0.0 copy-start
  31.7 3.9 %all-to-all-done.1.code_ref = bf16[16,32,128]{2,1,0:T(8,128)(2,1)S(1)} async-done(((bf16[16,32,128]{2,1,0:T(8,128)(2,1)}), bf16[16,32,128]{2,1,0:T(8,128)(2,1)S(1)}, u32[]{:S(2)}, u32[]{:S(2)}) %all-to-all-start.1) | async-done | bytes 131104 | tf_op jit(solution)/shard_map/all_to_all | solution.py:229
  35.6 0.0 copy-done
  35.6 1.6 %shard_map.74 = bf16[64,64,128]{2,1,0:T(8,128)(2,1)} custom-call(s32[4,64]{1,0:T(4,128)S(1)} %bitcast.12, bf16[16,32,128]{2,1,0:T(8,128)(2,1)S(1)} %all-to-all-done.1.code_ref, bf16[16,64,256]{2,1,0:T(8,128)(2,1)S(1)} %get-tuple-element.15.spectra_ref, bf16[16,256,128]{2,1,0:T(8,128)(2,1)S(1)} %shard_map.73.matrix_ref), custom_call_target="tpu_custom_call" | custom-call | flops 67108864 | bytes 1572864 | tf_op jit(solution)/shard_map/pallas_call | solution.py:133
  37.3 15.6 %all-to-all-start.2 = ((bf16[64,64,128]{2,1,0:T(8,128)(2,1)}), bf16[64,64,128]{2,1,0:T(8,128)(2,1)S(1)}, u32[]{:S(2)}, u32[]{:S(2)}) async-start(bf16[64,64,128]{2,1,0:T(8,128)(2,1)} %shard_map.74), calls=%async_computation.2 | async-start | bytes 2097152 | tf_op jit(solution)/shard_map/all_to_all | solution.py:229
  53.5 0.0 copy-start.4
  53.5 41.9 %all-to-all-done.2.held_ref = bf16[64,64,128]{2,1,0:T(8,128)(2,1)S(1)} async-done(((bf16[64,64,128]{2,1,0:T(8,128)(2,1)}), bf16[64,64,128]{2,1,0:T(8,128)(2,1)S(1)}, u32[]{:S(2)}, u32[]{:S(2)}) %all-to-all-start.2) | async-done | bytes 1048608 | tf_op jit(solution)/shard_map/all_to_all | solution.py:229
  95.4 0.0 copy-done.4
  95.4 2.4 %shard_map.75 = f32[6,64,64]{2,1,0:T(8,128)} custom-call(s32[2,6]{1,0:T(2,128)S(1)} %bitcast.14, s32[1]{0:T(128)S(6)} %copy.12.count_any, bf16[64,64,128]{2,1,0:T(8,128)(2,1)S(1)} %all-to-all-done.2.held_ref), custom_call_target="tpu_custom_call" | custom-call | flops 402653184 | bytes 1048576 | tf_op jit(solution)/shard_map/pallas_call | solution.py:202
  (3 shorter events, 0.0 us)
Async XLA Ops:
  12.9 15.9 %copy-start.3 = (s32[64]{0:T(128)S(1)}, s32[64]{0:T(128)}, u32[]{:S(2)}) copy-start(s32[64]{0:T(128)} %param.10) | copy-start | bytes 772
  12.9 22.8 %all-to-all-start.1 = ((bf16[16,32,128]{2,1,0:T(8,128)(2,1)}), bf16[16,32,128]{2,1,0:T(8,128)(2,1)S(1)}, u32[]{:S(2)}, u32[]{:S(2)}) async-start(bf16[16,32,128]{2,1,0:T(8,128)(2,1)} %broadcast_in_dim.18), calls=%async_computation.1 | async-start | bytes 262144 | tf_op jit(solution)/shard_map/all_to_all | solution.py:229
  28.7 0.7 copy-start.1
  28.7 0.7 copy-start.2
  31.7 4.0 %copy-start = (s32[64,4]{0,1:T(4,128)S(1)}, s32[64,4]{0,1:T(4,128)}, u32[]{:S(2)}) copy-start(s32[64,4]{0,1:T(4,128)} %param.11) | copy-start | bytes 3076
  37.3 58.2 %all-to-all-start.2 = ((bf16[64,64,128]{2,1,0:T(8,128)(2,1)}), bf16[64,64,128]{2,1,0:T(8,128)(2,1)S(1)}, u32[]{:S(2)}, u32[]{:S(2)}) async-start(bf16[64,64,128]{2,1,0:T(8,128)(2,1)} %shard_map.74), calls=%async_computation.2 | async-start | bytes 2097152 | tf_op jit(solution)/shard_map/all_to_all | solution.py:229
  53.5 41.9 %copy-start.4 = (s32[1,6,2]{1,2,0:T(2,128)S(1)}, s32[1,6,2]{1,2,0:T(2,128)}, u32[]{:S(2)}) copy-start(s32[1,6,2]{1,2,0:T(2,128)} %param.12) | copy-start | bytes 148

commit v8 on v7

--- a/solution.py
+++ b/solution.py
@@ -97,7 +97,7 @@
     held = ids_ref.shape[0]
     steps, per_step = chunk.shape[0], chunk.shape[1]
     groups = decode(code_ref[...]).reshape(-1, subarrays, width // 2)
-    scale = lax.rsqrt(jnp.sum(groups, axis=0) / count + eps)
+    scale = lax.rsqrt(jnp.sum(groups, axis=0) * (1.0 / count) + eps)
     scale = jnp.concatenate([scale, scale], axis=1)
     for n in range(bins):
         white = (spectra_ref[n].astype(jnp.float32) * scale).astype(jnp.bfloat16)
@@ -192,7 +192,7 @@
         copy.wait()
     for p in range(power_ref.shape[0]):
         row = pl.multiple_of(slots_ref[0, p] * half, half)
-        power = picked[slots_ref[1, p] - 1, pl.ds(row, half), :] / (bins * records)
+        power = picked[slots_ref[1, p] - 1, pl.ds(row, half), :] * (1.0 / (bins * records))
         power_ref[p] = jnp.where(p < count_ref[0], power, 0.0)
 
 

time: 98.2 us -> 98.2 us (level)
  no operation moved by 1% of the time
where the time goes in v8:
time: 98.2 us; the launch traced here: 97.9 us
  waiting for transfers between devices  45.8 us (47%)
  starting transfers between devices  31.4 us (32%)
  blocking collectives  10.8 us (11%)
  Pallas kernels  6.33 us (6%)
  local copies, waits for them, and re-layouts  1.36 us (1%)
  other arithmetic  1.33 us (1%)
    all_to_all x2, waiting for transfers between devices, exchange(): lax.all_to_all(blocks, 'sub', split_axis=0, concat_axis=0, tiled=True, ax...  45.8 us
    all_to_all x2, starting transfers between devices, exchange(): lax.all_to_all(blocks, 'sub', split_axis=0, concat_axis=0, tiled=True, ax...  31.4 us
    all_to_all x1, blocking collectives, exchange(): lax.all_to_all(blocks, 'sub', split_axis=0, concat_axis=0, tiled=True, ax...  10.8 us
    pallas_call x1, Pallas kernels, pair_powers(): pl.pallas_call(functools.partial(pair_kernel, bins), out_shape=jax.ShapeD...  2.41 us
    pallas_call x1, Pallas kernels, steering(): pl.pallas_call(steering_kernel, out_shape=jax.ShapeDtypeStruct((bins, 2 *...  2.28 us
  transfers between devices with their start and end apart: 2, of which 2 were waited for; matrix products, arithmetic and copies ran while one was open for 0% of the time, Pallas kernels for 2%

profile of v8, /device:TPU:6, one launch (start us, length us, event | category | flops | bytes accessed | tf_op | source)
XLA Modules:
  0.0 97.9 jit_solution(4937553174015726488)
XLA Ops:
  0.0 1.2 %copy_bitcast_fusion = (bf16[16,64,256]{2,1,0:T(8,128)(2,1)S(1)}, f32[64,16,256]{2,0,1:T(8,128)S(1)}) fusion(bf16[1,64,16,256]{3,2,1,0:T(8,128)(2,1)} %param.7), kind=kLoop, calls=%fused_computation.5 | loop fusion | flops 262144 | bytes 2097152 | tf_op jit(solution)/shard_map/transpose | solution.py:254
  1.2 0.1 fusion.1
  1.3 10.8 %all_to_all.15 = f32[8,32,128]{2,1,0:T(8,128)S(1)} all-to-all(f32[8,32,128]{2,1,0:T(8,128)S(1)} %bitcast.15), channel_id=1, replica_groups={{2,3,0,1,6,7,4,5},{10,11,8,9,14,15,12,13},{18,19,16,17,22,23,20,21},{26..., dimensions={0} | all-to-all | bytes 262144 | tf_op jit(solution)/shard_map/all_to_all | solution.py:229
  12.2 0.7 broadcast_in_dim.18
  12.9 0.0 copy-start.3
  12.9 15.8 %all-to-all-start.1 = ((bf16[16,32,128]{2,1,0:T(8,128)(2,1)}), bf16[16,32,128]{2,1,0:T(8,128)(2,1)S(1)}, u32[]{:S(2)}, u32[]{:S(2)}) async-start(bf16[16,32,128]{2,1,0:T(8,128)(2,1)} %broadcast_in_dim.18), calls=%async_computation.1 | async-start | bytes 262144 | tf_op jit(solution)/shard_map/all_to_all | solution.py:229
  28.7 0.0 copy-start.1
  28.7 0.0 copy-start.2
  28.7 0.0 copy-done.3
  28.7 0.6 copy-done.1
  29.4 0.0 copy-done.2
  29.4 2.3 %shard_map.73.matrix_ref = bf16[16,256,128]{2,1,0:T(8,128)(2,1)S(1)} custom-call(f32[16]{0:T(128)S(1)} %copy-done.2, f32[2,128]{1,0:T(2,128)S(1)} %copy-done.1, s32[1,64]{1,0:T(1,128)S(1)} %bitcast.13), custom_call_target="tpu_custom_call" | custom-call | flops 7864320 | bytes 1048576 | tf_op jit(solution)/shard_map/pallas_call | solution.py:60
  31.7 0.0 copy-start
  31.7 3.9 %all-to-all-done.1.code_ref = bf16[16,32,128]{2,1,0:T(8,128)(2,1)S(1)} async-done(((bf16[16,32,128]{2,1,0:T(8,128)(2,1)}), bf16[16,32,128]{2,1,0:T(8,128)(2,1)S(1)}, u32[]{:S(2)}, u32[]{:S(2)}) %all-to-all-start.1) | async-done | bytes 131104 | tf_op jit(solution)/shard_map/all_to_all | solution.py:229
  35.6 0.0 copy-done
  35.6 1.6 %shard_map.74 = bf16[64,64,128]{2,1,0:T(8,128)(2,1)} custom-call(s32[4,64]{1,0:T(4,128)S(1)} %bitcast.12, bf16[16,32,128]{2,1,0:T(8,128)(2,1)S(1)} %all-to-all-done.1.code_ref, bf16[16,64,256]{2,1,0:T(8,128)(2,1)S(1)} %get-tuple-element.15.spectra_ref, bf16[16,256,128]{2,1,0:T(8,128)(2,1)S(1)} %shard_map.73.matrix_ref), custom_call_target="tpu_custom_call" | custom-call | flops 67108864 | bytes 1572864 | tf_op jit(solution)/shard_map/pallas_call | solution.py:133
  37.3 15.6 %all-to-all-start.2 = ((bf16[64,64,128]{2,1,0:T(8,128)(2,1)}), bf16[64,64,128]{2,1,0:T(8,128)(2,1)S(1)}, u32[]{:S(2)}, u32[]{:S(2)}) async-start(bf16[64,64,128]{2,1,0:T(8,128)(2,1)} %shard_map.74), calls=%async_computation.2 | async-start | bytes 2097152 | tf_op jit(solution)/shard_map/all_to_all | solution.py:229
  53.5 0.0 copy-start.4
  53.5 41.9 %all-to-all-done.2.held_ref = bf16[64,64,128]{2,1,0:T(8,128)(2,1)S(1)} async-done(((bf16[64,64,128]{2,1,0:T(8,128)(2,1)}), bf16[64,64,128]{2,1,0:T(8,128)(2,1)S(1)}, u32[]{:S(2)}, u32[]{:S(2)}) %all-to-all-start.2) | async-done | bytes 1048608 | tf_op jit(solution)/shard_map/all_to_all | solution.py:229
  95.4 0.0 copy-done.4
  95.4 2.4 %shard_map.75 = f32[6,64,64]{2,1,0:T(8,128)} custom-call(s32[2,6]{1,0:T(2,128)S(1)} %bitcast.14, s32[1]{0:T(128)S(6)} %copy.12.count_any, bf16[64,64,128]{2,1,0:T(8,128)(2,1)S(1)} %all-to-all-done.2.held_ref), custom_call_target="tpu_custom_call" | custom-call | flops 402653184 | bytes 1048576 | tf_op jit(solution)/shard_map/pallas_call | solution.py:202
  (3 shorter events, 0.0 us)
Async XLA Ops:
  12.9 15.9 %copy-start.3 = (s32[64]{0:T(128)S(1)}, s32[64]{0:T(128)}, u32[]{:S(2)}) copy-start(s32[64]{0:T(128)} %param.10) | copy-start | bytes 772
  12.9 22.8 %all-to-all-start.1 = ((bf16[16,32,128]{2,1,0:T(8,128)(2,1)}), bf16[16,32,128]{2,1,0:T(8,128)(2,1)S(1)}, u32[]{:S(2)}, u32[]{:S(2)}) async-start(bf16[16,32,128]{2,1,0:T(8,128)(2,1)} %broadcast_in_dim.18), calls=%async_computation.1 | async-start | bytes 262144 | tf_op jit(solution)/shard_map/all_to_all | solution.py:229
  28.7 0.7 copy-start.1
  28.7 0.7 copy-start.2
  31.7 4.0 %copy-start = (s32[64,4]{0,1:T(4,128)S(1)}, s32[64,4]{0,1:T(4,128)}, u32[]{:S(2)}) copy-start(s32[64,4]{0,1:T(4,128)} %param.11) | copy-start | bytes 3076
  37.3 58.2 %all-to-all-start.2 = ((bf16[64,64,128]{2,1,0:T(8,128)(2,1)}), bf16[64,64,128]{2,1,0:T(8,128)(2,1)S(1)}, u32[]{:S(2)}, u32[]{:S(2)}) async-start(bf16[64,64,128]{2,1,0:T(8,128)(2,1)} %shard_map.74), calls=%async_computation.2 | async-start | bytes 2097152 | tf_op jit(solution)/shard_map/all_to_all | solution.py:229
  53.5 41.9 %copy-start.4 = (s32[1,6,2]{1,2,0:T(2,128)S(1)}, s32[1,6,2]{1,2,0:T(2,128)}, u32[]{:S(2)}) copy-start(s32[1,6,2]{1,2,0:T(2,128)} %param.12) | copy-start | bytes 148
